TPU v7x, 32 devices: a whole 2x2x4 slice. The times are simulated.
32 devices in a mesh: groups: 2 (over x), tiles: 8 (over z, y), sub: 2 (over core).
Axes of the slice: x: 2, y: 2, z: 4, core: 2. Of those that a mesh axis runs over, the one named last changes fastest.
Arguments:
- density: float32 [768, 1536], P(('groups', 'tiles'), 'sub'), parts along dimension 0, may hold values from 0.8 to 1.2
- momentum: float32 [3, 768, 1536], P(None, ('groups', 'tiles'), 'sub'), parts along dimension 1, may hold values from -0.4 to 0.4
- stress: float32 [6, 768, 1536], P(None, ('groups', 'tiles'), 'sub'), parts along dimension 1, may hold values from -0.4 to 0.4
- red_density: float32 [768, 1536], P(('groups', 'tiles'), 'sub'), parts along dimension 0, may hold values from 0.1 to 0.8
- solid: int32 [768, 1536], P(('groups', 'tiles'), 'sub'), parts along dimension 0, may hold values 0 or 1
- widths: int32 [16], P('groups'), parts along dimension 0, may hold values from 1 to 3, 16 in all
Outputs:
- density_next: float32 [768, 1536], P(('groups', 'tiles'), 'sub'), parts along dimension 0
- momentum_next: float32 [3, 768, 1536], P(None, ('groups', 'tiles'), 'sub'), parts along dimension 1
- stress_next: float32 [6, 768, 1536], P(None, ('groups', 'tiles'), 'sub'), parts along dimension 1
- red_next: float32 [768, 1536], P(('groups', 'tiles'), 'sub'), parts along dimension 0
There are 2 independent parts, one for each index of `groups`. A program takes and returns all parts, laid end to end along the dimension named above; each array names one. Nothing has to cross between parts.
Inputs may be any that keep to these rules, and one draw needn't show every extreme that they name: Device k along tiles owns the tile columns from widths[0] + ... + widths[k-1] on, widths[k] of them, alike in every part of sub; they sum to 16, and one equals 3. 1 marks a solid cell, 0 a pore cell.
All inputs are finite; a program needn't handle non-finite values. No bound on the sum of `solid` on one device may be relied on, other than what follows from the above.
Results may differ from a plain program's by a relative error of at most 0.0003.
Values sent between devices are 32-bit elements; how exact they have to be, the bound alone decides.
No kernel may reach another device: no remote copies, remote signals or barrier semaphores. Data moves between devices by JAX's collectives and lax.ppermute only.
A program may use at most 64 MiB of HBM per device.

v0:
```python
import functools

import jax
import jax.numpy as jnp
from jax import lax
from jax.experimental import pallas as pl
from jax.experimental.pallas import tpu as pltpu
from jax.sharding import PartitionSpec as P

TILE = 16
STEPS = 2
RELAX_TIME = 0.8
SURFACE = 0.1
SEPARATION = 0.7

LANES = 128
SUBLANES = 8
FULL = 3
HALO = FULL + 1
FIELDS = 11
PLANES = FIELDS + 1
MOVED = 19
REDS = 5
HELD = MOVED + 1
RIM = 4
SLAB = HALO + 2 * RIM
OWN_TILES = SUBLANES - 2
GROUP = 4
PACKED = FULL * PLANES // GROUP * (GROUP - 1)
END_ROWS = (PACKED + 1) * SUBLANES
HALF = LANES // 2
ORDER = (0, 1, 2, 3, 10, 11, 4, 5, 6, 7, 8, 9)
PAIRS = PLANES // 2
PLACES = PLANES + 1
SPLIT = 4
KEPT = 2
COLOUR_BLOCK = (16, 1)
COLLIDE_BLOCK = (8, 1)
ARRIVE_BLOCK = (8, 1)
VMEM = pl.BlockSpec(memory_space=pltpu.VMEM)
SMEM = pl.BlockSpec(memory_space=pltpu.SMEM)
ANY = pl.BlockSpec(memory_space=pl.ANY)
HBM = pl.BlockSpec(memory_space=pltpu.HBM)


class Rows:
    def __init__(self, parts):
        self.parts = parts

    def _with(self, other, operation):
        others = other.parts if isinstance(other, Rows) else [other] * len(self.parts)
        return Rows([operation(one, two) for one, two in zip(self.parts, others)])

    def __add__(self, other):
        return self._with(other, lambda one, two: one + two)

    def __sub__(self, other):
        return self._with(other, lambda one, two: one - two)

    def __rsub__(self, other):
        return self._with(other, lambda one, two: two - one)

    def __mul__(self, other):
        return self._with(other, lambda one, two: one * two)

    def __or__(self, other):
        return self._with(other, lambda one, two: one | two)

    def __eq__(self, other):
        return self._with(other, lambda one, two: one == two)

    __radd__, __rmul__, __ror__ = __add__, __mul__, __or__

    def each(self, operation):
        return Rows([operation(part) for part in self.parts])


def select(mask, yes, no):
    count = max(len(item.parts) for item in (mask, yes, no) if isinstance(item, Rows))
    columns = [
        item.parts if isinstance(item, Rows) else [item] * count for item in (mask, yes, no)
    ]
    return Rows([jnp.where(*row) for row in zip(*columns)])


def roll_lanes(values, amount):
    return values.each(lambda part: pltpu.roll(part, amount % LANES, 1))


def roll_sublanes(values, amount):
    return values.each(lambda part: pltpu.roll(part, amount % SUBLANES, 0))


class Geometry:
    def __init__(self, info, own_tiles):
        live, first, last, sub_index = info[0], info[1], info[2], info[3]
        self.live = live
        self.low_row = jnp.where(first == 1, 0, -1000)
        self.high_row = jnp.where(last == 1, live, 1000)
        shape = (SUBLANES, LANES)
        lane = lax.broadcasted_iota(jnp.int32, shape, 1)
        tile = lax.broadcasted_iota(jnp.int32, shape, 0)
        depth = lane & (TILE - 1)
        low_part = sub_index == 0
        high_part = sub_index == 1
        z_walls = {1: depth == 0, -1: depth == TILE - 1}
        y_walls = {
            1: (tile == 1) & (lane < TILE) & low_part,
            -1: (tile == own_tiles) & (lane >= LANES - TILE) & high_part,
        }
        self.walls = {(0, vel_z): wall for vel_z, wall in z_walls.items()}
        for vel_y, y_wall in y_walls.items():
            self.walls[vel_y, 0] = y_wall
            for vel_z, z_wall in z_walls.items():
                self.walls[vel_y, vel_z] = y_wall | z_wall
        own = (tile >= 1) & (tile <= own_tiles)
        self.domain = own | ((tile == own_tiles + 1) & low_part) | ((tile == 0) & high_part)
        self.first_lanes = lane < TILE
        self.last_lanes = lane >= LANES - TILE

    def from_low_y(self, values):
        return roll_lanes(select(self.last_lanes, roll_sublanes(values, 1), values), TILE)

    def from_high_y(self, values):
        return roll_lanes(select(self.first_lanes, roll_sublanes(values, -1), values), -TILE)

    def from_low_z(self, values):
        return select(self.walls[0, 1], 0.0, roll_lanes(values, 1))

    def from_high_z(self, values):
        return select(self.walls[0, -1], 0.0, roll_lanes(values, -1))


def flat_rows(row, count, tile_offset=0):
    start = row * SUBLANES
    if not isinstance(start, int):
        start = pl.multiple_of(start, SUBLANES)
    return pl.ds(start + tile_offset, count * SUBLANES)


class ByRow:
    def __init__(self, ref):
        self.ref = ref


def by_row(rows, count):
    return jax.ShapeDtypeStruct((rows, count * SUBLANES, LANES), jnp.float32)


def place_of(ref, index, row, tile_offset=0):
    if isinstance(ref, ByRow):
        return ref.ref, row, pl.ds(index * SUBLANES + tile_offset, SUBLANES)
    return ref, index, flat_rows(row, 1, tile_offset)


def read_row(ref, index, row, tile_offset=0):
    ref, first, second = place_of(ref, index, row, tile_offset)
    return ref[first, second, :]


def write_row(ref, index, row, values):
    ref, first, second = place_of(ref, index, row)
    ref[first, second, :] = values


class Block:
    def __init__(self, geometry, spans, inner=False, store_rows=None):
        self.spans = spans
        self.store_rows = store_rows or [local for row, local, count in spans]
        rows = [row + extra for row, local, count in spans for extra in range(count)]
        self.inner = inner
        rows = [row + extra for row, local, count in spans for extra in range(count)]
        if inner:
            self.x_walls = {}
            self.valid = geometry.domain
            self.kinds = [0]
            return
        ids = Rows([row + jnp.zeros((SUBLANES, LANES), jnp.int32) for row in rows])
        self.x_walls = {1: ids == geometry.low_row, -1: ids == geometry.high_row - 1}
        self.valid = ids.each(
            lambda part: geometry.domain & (part >= geometry.low_row) & (part < geometry.high_row)
        )
        self.kinds = [
            jnp.where(row == geometry.low_row, 1, 0) + jnp.where(row == geometry.high_row - 1, 2, 0)
            for row in rows
        ]

    def load(self, ref, index, offset=0, tile_offset=0):
        return Rows([
            read_row(ref, index, local + offset + extra, tile_offset)
            for row, local, count in self.spans
            for extra in range(count)
        ])

    def store(self, ref, index, values):
        targets = [
            target + extra
            for (row, local, count), target in zip(self.spans, self.store_rows)
            for extra in range(count)
        ]
        for target, part in zip(targets, values.parts):
            write_row(ref, index, target, part)

    def wall_terms(self, walls, position):
        terms = [walls[position, flat_rows(kind, 1), :] for kind in self.kinds]
        return terms[0] if self.inner else Rows(terms)


def fill_wall_table(walls, geometry):
    one = jnp.ones((SUBLANES, LANES), jnp.float32)
    up_y, down_y, up_z, down_z = [
        jnp.where(geometry.walls[key], 0.0, one) for key in ((-1, 0), (1, 0), (0, -1), (0, 1))
    ]
    sum_y, sum_z = up_y + down_y, up_z + down_z
    for kind, (up_x, down_x) in enumerate(((1.0, 1.0), (1.0, 0.0), (0.0, 1.0))):
        sum_x = up_x + down_x
        around_x = 2.0 + sum_y + sum_z
        total = 12.0 + 2.0 * (sum_x + sum_y + sum_z) + sum_x * (sum_y + sum_z) + sum_y * sum_z
        rows = (
            (up_x - down_x) * around_x,
            (up_y - down_y) * (2.0 + sum_x + sum_z),
            (up_z - down_z) * (2.0 + sum_x + sum_y),
            36.0 - total,
        )
        for position, row in enumerate(rows):
            walls[position, flat_rows(kind, 1), :] = row


VELOCITIES = tuple(
    tuple(sign if axis == place else 0 for place in range(3)) for axis in range(3) for sign in (1, -1)
) + tuple(
    tuple({a: one, b: two}.get(place, 0) for place in range(3))
    for a, b in ((0, 1), (0, 2), (1, 2))
    for one, two in ((1, 1), (-1, -1), (1, -1), (-1, 1))
)
VELOCITIES = ((0, 0, 0),) + VELOCITIES


def colour_stage(block, geometry, fields, colours):
    density = block.load(fields, 0)
    red = block.load(fields, 10)
    colour = select(block.valid, 2.0 * red - density, 0.0)
    along_y = geometry.from_low_y(colour) + geometry.from_high_y(colour)
    along_z = geometry.from_low_z(colour) + geometry.from_high_z(colour)
    block.store(colours, 0, colour)
    block.store(colours, 1, 2.0 * colour + (along_y + along_z))
    block.store(colours, 2, along_y)
    block.store(colours, 3, along_z)


def collide_stage(block, geometry, fields, solids, colours, walls, state):
    relaxing = 1.0 - 1.0 / RELAX_TIME
    third = 1.0 / 3.0
    colour = block.load(colours, 0)
    doubled = 2.0 * colour + (block.load(colours, 0, -1) + block.load(colours, 0, 1))
    term_y = doubled + block.load(colours, 3)
    term_z = doubled + block.load(colours, 2)
    grad_x = block.load(colours, 1, 1) - block.load(colours, 1, -1)
    grad_y = geometry.from_high_y(term_y) - geometry.from_low_y(term_y)
    grad_z = geometry.from_high_z(term_z) - geometry.from_low_z(term_z)
    if not block.inner:
        grad_x = grad_x - block.wall_terms(walls, 0) * colour
    grad_y = grad_y - block.wall_terms(walls, 1) * colour
    grad_z = grad_z - block.wall_terms(walls, 2) * colour

    fluid = block.load(solids, PLANES - 1) == 0.0
    density = block.load(fields, 0)
    red = block.load(fields, 10)
    flux = [block.load(fields, 1 + axis) for axis in range(3)]
    stress = [block.load(fields, 4 + part) for part in range(6)]
    square_xx, square_yy, square_zz = grad_x * grad_x, grad_y * grad_y, grad_z * grad_z
    square = square_xx + square_yy + square_zz
    inverse = select(fluid, (1.0 + square * (1.0 / 144.0)).each(lax.rsqrt), 0.0)
    trace = third * square
    strength = (SURFACE / (8.0 * 144.0)) * inverse
    keep = select(fluid, relaxing / 8.0, 1.0 / 8.0)
    eighths = [0.125 * part for part in flux]
    own = [
        eighths[axis] * flux[axis] + (keep * stress[axis] + strength * (squared - trace))
        for axis, squared in enumerate((square_xx, square_yy, square_zz))
    ]
    strength, keep = 2.0 * strength, 2.0 * keep
    quarters = [2.0 * part for part in eighths[:2]]
    grads = (grad_x, grad_y, grad_z)
    cross = [
        quarters[a] * flux[b] + (keep * stress[3 + plane] + strength * (grads[a] * grads[b]))
        for plane, (a, b) in enumerate(((0, 1), (0, 2), (1, 2)))
    ]
    base = density * (1.0 / 36.0) - third * (own[0] + own[1] + own[2])
    sign = select(fluid, 1.0 / 12.0, -1.0 / 12.0)
    run = [sign * part for part in flux]
    mixing = ((SEPARATION / 144.0) * red) * ((density - red) * inverse)
    red_run = [0.5 * part + mixing * grad for part, grad in zip(run, grads)]
    moved, reds = state
    block.store(moved, 0, 12.0 * base)
    straight = [base + part for part in own]
    for axis in range(3):
        middle = 2.0 * straight[axis]
        swing = 2.0 * run[axis]
        block.store(moved, 1 + 2 * axis, middle + swing)
        block.store(moved, 2 + 2 * axis, middle - swing)
    for plane, (a, b) in enumerate(((0, 1), (0, 2), (1, 2))):
        middle = straight[a] + own[b]
        same, other = middle + cross[plane], middle - cross[plane]
        along, against = run[a] + run[b], run[a] - run[b]
        first = 7 + 4 * plane
        block.store(moved, first, same + along)
        block.store(moved, first + 1, same - along)
        block.store(moved, first + 2, other + against)
        block.store(moved, first + 3, other - against)

    red_base = select(block.valid, red * (1.0 / 36.0), 0.0)
    red_run = [select(block.valid, part, 0.0) for part in red_run]
    block.store(reds, 0, red_base)
    block.store(reds, 1, red_base + red_run[0])
    block.store(reds, 2, red_base - red_run[0])
    block.store(reds, 3, red_run[1])
    block.store(reds, 4, red_run[2])


def arrive_stage(block, geometry, walls, state, fields):
    third = 1.0 / 3.0
    moved, reds = state
    own = [None] * MOVED

    def here(direction):
        if own[direction] is None:
            own[direction] = block.load(moved, direction)
        return own[direction]

    def arrived(direction, opposite):
        vel_x, vel_y, vel_z = VELOCITIES[direction]
        values = here(direction) if vel_x == 0 else block.load(moved, direction, -vel_x)
        if vel_y != 0:
            beside = block.load(moved, direction, -vel_x, -vel_y)
            leaving = geometry.last_lanes if vel_y == 1 else geometry.first_lanes
            values = select(leaving, beside, values)
        if vel_y != 0 or vel_z != 0:
            values = roll_lanes(values, TILE * vel_y + vel_z)
        masks = []
        if vel_x in block.x_walls:
            masks.append(block.x_walls[vel_x])
        if (vel_y, vel_z) in geometry.walls:
            masks.append(geometry.walls[vel_y, vel_z])
        if not masks:
            return values
        wall = functools.reduce(lambda one, two: one | two, masks)
        return select(wall, here(opposite), values)

    red = block.load(reds, 0)
    red_y = block.load(reds, 3)
    red_z = block.load(reds, 4)
    from_x = block.load(reds, 1, -1) + block.load(reds, 2, 1)
    spread = 2.0 * red + from_x
    spread_y = 2.0 * red_y + (block.load(reds, 3, -1) + block.load(reds, 3, 1))
    spread_z = 2.0 * red_z + (block.load(reds, 4, -1) + block.load(reds, 4, 1))
    up_y, down_y = red + red_y, red - red_y
    low_y = (
        (spread + spread_y)
        + geometry.from_low_z(up_y + red_z)
        + geometry.from_high_z(up_y - red_z)
    )
    high_y = (
        (spread - spread_y)
        + geometry.from_low_z(down_y + red_z)
        + geometry.from_high_z(down_y - red_z)
    )
    bounced = (
        block.wall_terms(walls, 3) * red
        - block.wall_terms(walls, 1) * red_y
        - block.wall_terms(walls, 2) * red_z
    )
    if not block.inner:
        bounced = bounced - block.wall_terms(walls, 0) * (block.load(reds, 1) - red)
    red_total = (
        12.0 * red
        + 2.0 * from_x
        + geometry.from_low_z(spread + spread_z)
        + geometry.from_high_z(spread - spread_z)
        + geometry.from_low_y(low_y)
        + geometry.from_high_y(high_y)
        + bounced
    )
    rest = here(0)
    sums, diffs = [], []
    for axis in range(3):
        up = arrived(1 + 2 * axis, 2 + 2 * axis)
        down = arrived(2 + 2 * axis, 1 + 2 * axis)
        sums.append(up + down)
        diffs.append(up - down)
    total = rest + sums[0] + sums[1] + sums[2]
    cross = []
    for plane, (a, b) in enumerate(((0, 1), (0, 2), (1, 2))):
        first = 7 + 4 * plane
        parts = [arrived(first + offset, first + (offset ^ 1)) for offset in range(4)]
        same, other = parts[0] + parts[1], parts[2] + parts[3]
        along, against = parts[0] - parts[1], parts[2] - parts[3]
        both = same + other
        cross.append(same - other)
        total = total + both
        sums[a], sums[b] = sums[a] + both, sums[b] + both
        diffs[a], diffs[b] = diffs[a] + (along + against), diffs[b] + (along - against)
    shared = third * total
    block.store(fields, 0, total)
    for axis in range(3):
        block.store(fields, 1 + axis, diffs[axis])
        block.store(fields, 4 + axis, sums[axis] - shared - diffs[axis] * diffs[axis])
    for plane, (a, b) in enumerate(((0, 1), (0, 2), (1, 2))):
        block.store(fields, 7 + plane, cross[plane] - diffs[a] * diffs[b])
    block.store(fields, 10, red_total)


def over_rows(geometry, first, size, blocks, stage):
    trip = size * blocks
    rest = -2 * first % trip
    assert TILE % trip == 0 and rest % min(size, rest or size) == 0

    def run(start, count, step_size):
        for offset in range(0, count, step_size):
            row = start + offset
            stage(Block(geometry, [(row, row, step_size)], inner=True))

    def step(index, carry):
        run(first + index * trip, trip, size)
        return carry

    trips = (geometry.live - 2 * first - rest) // trip
    lax.fori_loop(0, trips, step, 0)
    if rest:
        run(geometry.live - first - rest, rest, min(size, rest))


def block_tiles():
    return lax.broadcasted_iota(jnp.int32, (SUBLANES, LANES), 0)


def roll_tiles(block, amount):
    return pltpu.roll(block, amount % SUBLANES, 0)


def pack_blocks(blocks):
    tiles, rest = block_tiles(), blocks[GROUP - 1]
    packed = []
    for number, block in enumerate(blocks[: GROUP - 1]):
        low, high = 2 * number + 1, 2 * number + 2
        block = jnp.where(tiles == 0, roll_tiles(rest, -low), block)
        packed.append(jnp.where(tiles == SUBLANES - 1, roll_tiles(rest, SUBLANES - 1 - high), block))
    return packed


def unpack_blocks(packed):
    tiles, rest = block_tiles(), None
    for number, block in enumerate(packed):
        low, high = 2 * number + 1, 2 * number + 2
        part = jnp.where(tiles == low, roll_tiles(block, low), roll_tiles(block, high - SUBLANES + 1))
        rest = part if rest is None else jnp.where(tiles >= low, part, rest)
    return list(packed) + [rest]


def flat_view(ref):
    rows, width, lanes = ref.shape
    return ref.reshape(rows * width, lanes)


def spread_tile(raw, raw_solid, index, row, target, target_row):
    source = raw_solid if index == FIELDS else raw.at[index]
    width = target.shape[1]
    for tile in range(OWN_TILES):
        values = source[pl.ds(row, SUBLANES), pl.ds(tile * LANES, LANES)].astype(jnp.float32)
        start = target_row * width + index * SUBLANES + 1 + tile
        flat_view(target)[pl.ds(start, SUBLANES, stride=width), :] = values


def load_kernel(
    tiles_count, density, momentum, stress, red, solid, widths,
    info, raw, raw_solid, packet, mine,
    first_tile, last_tile, held_widths, sems,
):
    row_count, flat_count = raw_solid.shape
    own_tiles = flat_count // LANES
    copies = [
        pltpu.make_async_copy(widths, held_widths, sems.at[0]),
        pltpu.make_async_copy(density, raw.at[0], sems.at[1]),
        pltpu.make_async_copy(momentum, raw.at[pl.ds(1, 3)], sems.at[2]),
        pltpu.make_async_copy(red, raw.at[10], sems.at[3]),
        pltpu.make_async_copy(solid, raw_solid, sems.at[4]),
        pltpu.make_async_copy(stress.at[pl.ds(0, 3)], raw.at[pl.ds(4, 3)], sems.at[5]),
        pltpu.make_async_copy(stress.at[pl.ds(3, 3)], raw.at[pl.ds(7, 3)], sems.at[6]),
    ]
    for copy in copies:
        copy.start()
    tiles_index, sub_index = lax.axis_index("tiles"), lax.axis_index("sub")
    low_part = sub_index == 0
    edge_start = pl.multiple_of(jnp.where(low_part, (own_tiles - 1) * LANES, 0), LANES)

    copies[0].wait()
    live = held_widths[tiles_index] * TILE
    info[0] = live
    info[1] = (tiles_index == 0).astype(jnp.int32)
    info[2] = (tiles_index == tiles_count - 1).astype(jnp.int32)
    info[3] = sub_index

    near_cut = lax.broadcasted_iota(jnp.int32, (SUBLANES, LANES), 1) < HALF
    near_cut = near_cut == jnp.logical_not(low_part)
    near_last = pl.multiple_of(live - SUBLANES, SUBLANES)
    edges = pl.ds(edge_start, LANES)

    def plane_of(index):
        return raw_solid if index == FIELDS else raw.at[index]

    def pack_edges(pair):
        here, there = [plane_of(index) for index in ORDER[2 * pair : 2 * pair + 2]]
        for row in range(0, row_count, SUBLANES):
            rows = pl.ds(row, SUBLANES)
            beside = pltpu.roll(there[rows, edges].astype(jnp.float32), HALF, 1)
            both = jnp.where(near_cut, here[rows, edges].astype(jnp.float32), beside)
            packet[pl.ds(END_ROWS + pair * row_count + row, SUBLANES), :] = both

    targets = ((packet, jnp.logical_not(low_part)), (mine, low_part))

    def row_of(use_last, index, number_first, number_last):
        first = read_row(ByRow(first_tile), index, number_first)
        last = read_row(ByRow(last_tile), index, number_last)
        return jnp.where(use_last, last, first)

    def pack_ends(group):
        for target, use_last in targets:
            blocks = []
            for number in range(group * GROUP, (group + 1) * GROUP):
                place, extra = divmod(number, FULL)
                blocks.append(row_of(use_last, ORDER[place], extra, SUBLANES - FULL + extra))
            for number, block in enumerate(pack_blocks(blocks)):
                place = (group * (GROUP - 1) + number) * SUBLANES
                target[pl.ds(place, SUBLANES), :] = block

    place = 0
    for copy, count in zip(copies[1:], (1, 3, 1, 1, 3, 3)):
        copy.wait()
        before, place = place, place + count
        for index in ORDER[before:place]:
            for target, row in ((first_tile, 0), (last_tile, near_last)):
                spread_tile(raw, raw_solid, index, row, target, 0)
        for pair in range(before // 2, place // 2):
            pack_edges(pair)
        for group in range(before * FULL // GROUP, place * FULL // GROUP):
            pack_ends(group)
    for target, use_last in targets:
        red_row, density_row = [
            row_of(use_last, index, FULL, SUBLANES - HALO) for index in (10, 0)
        ]
        target[pl.ds(PACKED * SUBLANES, SUBLANES), :] = 2.0 * red_row - density_row


def load_inputs(arrays, widths, tiles_count):
    row_count, flat_count = arrays[0].shape
    return pl.pallas_call(
        functools.partial(load_kernel, tiles_count),
        out_shape=[
            pltpu.SMEM((4,), jnp.int32),
            jax.ShapeDtypeStruct((FIELDS, row_count, flat_count), jnp.float32),
            jax.ShapeDtypeStruct((row_count, flat_count), jnp.int32),
            jax.ShapeDtypeStruct((END_ROWS + PAIRS * row_count, LANES), jnp.float32),
            jax.ShapeDtypeStruct((END_ROWS, LANES), jnp.float32),
        ],
        in_specs=[HBM] * 6,
        out_specs=[SMEM] + [VMEM] * 4,
        scratch_shapes=[
            pltpu.VMEM((SUBLANES, PLACES * SUBLANES, LANES), jnp.float32),
            pltpu.VMEM((SUBLANES, PLACES * SUBLANES, LANES), jnp.float32),
            pltpu.SMEM(widths.shape, jnp.int32),
            pltpu.SemaphoreType.DMA((7,)),
        ],
        compiler_params=pltpu.CompilerParams(vmem_limit_bytes=16 * 1024 * 1024),
        name="load",
    )(*[pltpu.with_memory_space_constraint(array, pltpu.HBM) for array in (*arrays, widths)])


def spread_kernel(raw, raw_solid, spread):
    for index in range(PLANES):
        for row in range(0, raw_solid.shape[0], SUBLANES):
            spread_tile(raw, raw_solid, index, row, spread, row)


def spread_rows(raw, raw_solid):
    row_count = raw_solid.shape[0]
    return pl.pallas_call(
        spread_kernel,
        out_shape=by_row(row_count, PLACES),
        in_specs=[VMEM, VMEM],
        out_specs=VMEM,
        compiler_params=pltpu.CompilerParams(vmem_limit_bytes=16 * 1024 * 1024),
        cost_estimate=pl.CostEstimate(flops=1_000_000, bytes_accessed=4_000_000, transcendentals=0),
        name="spread",
    )(raw, raw_solid)


def join_kernel(mine, packet, spread, ends):
    ends[pl.ds(0, END_ROWS), :] = mine[...]
    ends[pl.ds(END_ROWS, END_ROWS), :] = packet[pl.ds(0, END_ROWS), :]


def join_ends(mine, packet, spread):
    return pl.pallas_call(
        join_kernel,
        out_shape=jax.ShapeDtypeStruct((2 * END_ROWS, LANES), jnp.float32),
        in_specs=[VMEM, VMEM, ANY],
        out_specs=VMEM,
        compiler_params=pltpu.CompilerParams(vmem_limit_bytes=8 * 1024 * 1024),
        name="join",
    )(mine, packet, spread)


def beside_kernel(info, spread, packet, whole):
    low_part = info[3] == 0
    row_count, width = spread.shape[:2]
    flat = flat_view(whole)
    for pair in range(PAIRS):
        for row in range(0, row_count, SUBLANES):
            both = packet[pl.ds(END_ROWS + pair * row_count + row, SUBLANES), :]
            for place, values in ((2 * pair, both), (2 * pair + 1, pltpu.roll(both, HALF, 1))):
                index = ORDER[place]
                start = row * width + index * SUBLANES
                below = jnp.where(low_part, 0.0, values)
                above = jnp.where(low_part, values, 0.0)
                flat[pl.ds(start, SUBLANES, stride=width), :] = below
                flat[pl.ds(start + SUBLANES - 1, SUBLANES, stride=width), :] = above


def put_beside(info, spread, packet):
    return pl.pallas_call(
        beside_kernel,
        out_shape=jax.ShapeDtypeStruct(spread.shape, jnp.float32),
        in_specs=[SMEM, VMEM, VMEM],
        out_specs=VMEM,
        input_output_aliases={1: 0},
        compiler_params=pltpu.CompilerParams(vmem_limit_bytes=16 * 1024 * 1024),
        name="beside",
    )(info, pltpu.with_memory_space_constraint(spread, pltpu.VMEM), packet)


def keep_rows(slab, source, first, size, live):
    for slab_row, row in slab_rows(live, first, size):
        for extra in range(size):
            slab[slab_row + extra] = source[row + extra]


def slab_rows(live, first, size):
    mirrored = SLAB - first - size
    return [(first, first - HALO), (SLAB + mirrored, live - 2 * RIM + mirrored)]


def collide_rows(geometry, before, whole, first, colours, walls, state):
    over_rows(geometry, first - 1, *COLOUR_BLOCK, lambda block: colour_stage(
        block, geometry, before, colours))
    over_rows(geometry, first, *COLLIDE_BLOCK, lambda block: collide_stage(
        block, geometry, before, whole, colours, walls, state))


def tile_copies(pieces, outs, held_row, out_row, sems):
    held, rows = pl.ds(held_row, SUBLANES), pl.ds(out_row, SUBLANES)
    parts = (
        (pieces.at[0, held], outs[0].at[rows]),
        (pieces.at[pl.ds(1, 3), held], outs[1].at[:, rows]),
        (pieces.at[pl.ds(4, 6), held], outs[2].at[:, rows]),
        (pieces.at[10, held], outs[3].at[rows]),
    )
    return [
        pltpu.make_async_copy(source, target, sems.at[number])
        for number, (source, target) in enumerate(parts)
    ]


def gather_tiles(final, row, pieces, held_row):
    width = final.shape[1]
    start = row * width
    if not isinstance(start, int):
        start = pl.multiple_of(start, SUBLANES)
    for index in range(FIELDS):
        for tile in range(OWN_TILES):
            place = start + index * SUBLANES + 1 + tile
            pieces[index, pl.ds(held_row, SUBLANES), pl.ds(tile * LANES, LANES)] = flat_view(final)[
                pl.ds(place, SUBLANES, stride=width), :
            ]


def first_kernel(
    info, whole, moved_later, reds_later, final,
    moved_slab, reds_slab, fields_slab, moved_later_slab, reds_later_slab, final_slab,
    colours, walls, moved, reds, fields,
):
    state, later = (ByRow(moved), ByRow(reds)), (ByRow(moved_later), ByRow(reds_later))
    geometry = Geometry(info, OWN_TILES)
    live = geometry.live
    fill_wall_table(walls, geometry)
    collide_rows(geometry, ByRow(whole), ByRow(whole), 1, ByRow(colours), walls, state)
    over_rows(geometry, 2, *ARRIVE_BLOCK, lambda block: arrive_stage(
        block, geometry, walls, state, ByRow(fields)))
    keep_rows(moved_slab, moved, HALO + 1, KEPT, live)
    keep_rows(reds_slab, reds, HALO + 1, KEPT, live)
    keep_rows(fields_slab, fields, HALO + 2, KEPT, live)
    collide_rows(geometry, ByRow(fields), ByRow(whole), 3, ByRow(colours), walls, later)
    keep_rows(moved_later_slab, moved_later, HALO + 3, KEPT, live)
    keep_rows(reds_later_slab, reds_later, HALO + 3, KEPT, live)
    edges = slab_rows(live, HALO + RIM, RIM)
    rim = Block(geometry, [(row, row, RIM) for _, row in edges], True, [at for at, _ in edges])
    arrive_stage(rim, geometry, walls, later, ByRow(final_slab))

    def arrive_tile(tile, carry):
        row = tile * SUBLANES
        block = Block(geometry, [(row, row, SUBLANES)], inner=True)
        arrive_stage(block, geometry, walls, later, ByRow(final))
        return carry

    lax.fori_loop(1, jnp.minimum(SPLIT, live // SUBLANES - 1), arrive_tile, 0)


def second_kernel(
    info, moved, reds, earlier, arrived, density_out, momentum_out, stress_out, red_out,
    final, walls, pieces, zeros, sems,
):
    outs = (density_out, momentum_out, stress_out, red_out)
    row_tiles = density_out.shape[0] // SUBLANES
    state = (ByRow(moved), ByRow(reds))
    geometry = Geometry(info, OWN_TILES)
    live = geometry.live
    last = live // SUBLANES - 1
    fill_wall_table(walls, geometry)

    def copies_of(tile):
        row = pl.multiple_of(tile * SUBLANES, SUBLANES)
        return tile_copies(pieces, outs, row, row, sems.at[tile])

    def send_out(tile, source):
        row = pl.multiple_of(tile * SUBLANES, SUBLANES)
        gather_tiles(source, row, pieces, row)
        for copy in copies_of(tile):
            copy.start()

    def pass_on(tile, carry):
        send_out(tile, earlier)
        return carry

    def finish(tile, carry):
        row = tile * SUBLANES
        block = Block(geometry, [(row, row, SUBLANES)], inner=True)
        arrive_stage(block, geometry, walls, state, ByRow(final))
        send_out(tile, final)
        return carry

    def settle(tile, carry):
        for copy in copies_of(tile):
            copy.wait()
        return carry

    lax.fori_loop(1, jnp.minimum(SPLIT, last), pass_on, 0)
    zeros[...] = jnp.zeros(zeros.shape, zeros.dtype)
    dead = {}
    for tile in range(row_tiles):
        dead[tile] = tile_copies(zeros, outs, 0, tile * SUBLANES, sems.at[tile])

        @pl.when(tile * SUBLANES >= live)
        def _():
            for copy in dead[tile]:
                copy.start()

    lax.fori_loop(SPLIT, last, finish, 0)
    lax.fori_loop(1, last, settle, 0)
    for tile in range(row_tiles):

        @pl.when(tile * SUBLANES >= live)
        def _():
            for copy in dead[tile]:
                copy.wait()


def scratch_of(shape):
    return pltpu.VMEM(shape.shape, shape.dtype)


def pieces_of(rows, flat_count):
    return pltpu.VMEM((FIELDS, rows, flat_count), jnp.float32)


def run_first(info, whole):
    rows = whole.shape[0]
    shapes = [by_row(rows, count) for count in (HELD, REDS, FIELDS)]
    slabs = [by_row(2 * SLAB, count) for count in (HELD, REDS, FIELDS, HELD, REDS, FIELDS)]
    scratch = [by_row(rows, 4), by_row(4, 3)]
    scratch = scratch + [by_row(rows, count) for count in (HELD, REDS, FIELDS)]
    return pl.pallas_call(
        first_kernel,
        out_shape=shapes + slabs,
        in_specs=[SMEM, VMEM],
        out_specs=[VMEM] * 9,
        scratch_shapes=[scratch_of(shape) for shape in scratch],
        compiler_params=pltpu.CompilerParams(vmem_limit_bytes=24 * 1024 * 1024),
        cost_estimate=pl.CostEstimate(flops=20_000_000, bytes_accessed=8_000_000, transcendentals=0),
        name="first",
    )(info, whole)


def run_second(info, state, earlier, arrived, arrays):
    row_count, flat_count = arrays[0].shape
    return pl.pallas_call(
        second_kernel,
        out_shape=[jax.ShapeDtypeStruct(array.shape, jnp.float32) for array in arrays[:4]],
        in_specs=[SMEM] + [VMEM] * 3 + [ANY],
        out_specs=[ANY] * 4,
        scratch_shapes=[
            scratch_of(by_row(row_count, FIELDS)),
            scratch_of(by_row(4, 3)),
            pieces_of(row_count, flat_count),
            pieces_of(SUBLANES, flat_count),
            pltpu.SemaphoreType.DMA((row_count // SUBLANES, 4)),
        ],
        compiler_params=pltpu.CompilerParams(vmem_limit_bytes=24 * 1024 * 1024),
        cost_estimate=pl.CostEstimate(flops=20_000_000, bytes_accessed=8_000_000, transcendentals=0),
        name="second",
    )(info, *state, earlier, arrived)


def follow_kernel(ends, kept, out):
    out[pl.ds(PACKED * SUBLANES, 1), :] = jnp.zeros((1, LANES), jnp.float32)


def follow(ends, kept):
    return pl.pallas_call(
        follow_kernel,
        out_shape=jax.ShapeDtypeStruct(ends.shape, jnp.float32),
        in_specs=[VMEM, ANY],
        out_specs=VMEM,
        input_output_aliases={0: 0},
        compiler_params=pltpu.CompilerParams(vmem_limit_bytes=8 * 1024 * 1024),
        name="follow",
    )(pltpu.with_memory_space_constraint(ends, pltpu.VMEM), kept)


def outer_kernel(info, whole, arrived, passed, *refs):
    outs = refs[10:14]
    moved, reds, fields, moved_later, reds_later, final = refs[14:20]
    start_fields, colours, walls, pieces, sems = refs[20:]
    state, later = (ByRow(moved), ByRow(reds)), (ByRow(moved_later), ByRow(reds_later))
    geometry = Geometry(info, OWN_TILES)
    live = geometry.live
    low_part = info[3] == 0
    fill_wall_table(walls, geometry)

    def ends_of(ref, half):
        blocks = []
        for group in range(FULL * PLANES // GROUP):
            first = half * (PACKED + 1) + group * (GROUP - 1)
            packed = [ref[pl.ds((first + k) * SUBLANES, SUBLANES), :] for k in range(GROUP - 1)]
            blocks = blocks + unpack_blocks(packed)
        last = half * (PACKED + 1) + PACKED
        return blocks + [ref[pl.ds(last * SUBLANES, SUBLANES), :]]

    tiles = block_tiles()
    middle = (tiles >= 1) & (tiles <= OWN_TILES)

    def widened(own, other):
        beside = jnp.where(tiles == 0, roll_tiles(other, -OWN_TILES), roll_tiles(other, OWN_TILES))
        return jnp.where(geometry.domain, jnp.where(middle, own, beside), 0.0)

    straight = [widened(*pair) for pair in zip(ends_of(arrived, 0), ends_of(arrived, 1))]
    crossed = [widened(*pair) for pair in zip(ends_of(passed, 1), ends_of(passed, 0))]
    below = [jnp.where(low_part, *pair) for pair in zip(straight, crossed)]
    above = [jnp.where(low_part, *pair) for pair in zip(crossed, straight)]

    for number in range(FULL * PLANES):
        place, extra = divmod(number, FULL)
        index = ORDER[place]
        write_row(ByRow(start_fields), index, 1 + extra, below[number])
        write_row(ByRow(start_fields), index, 2 * SLAB - HALO + extra, above[number])
    for row, colour in ((0, below[-1]), (2 * SLAB - 1, above[-1])):
        write_row(ByRow(start_fields), 0, row, jnp.zeros((SUBLANES, LANES), jnp.float32))
        write_row(ByRow(start_fields), 10, row, 0.5 * colour)
    for slab_row, row in slab_rows(live, HALO, FULL):
        for extra in range(FULL):
            start_fields[slab_row + extra] = whole[row + extra]

    def block(first, count):
        return Block(geometry, [(row, at, count) for at, row in slab_rows(live, first, count)])

    held, solids, marks = ByRow(fields), ByRow(start_fields), ByRow(colours)
    colour_stage(block(0, 6), geometry, solids, marks)
    collide_stage(block(1, 4), geometry, solids, solids, marks, walls, state)
    arrive_stage(block(2, 4), geometry, walls, state, held)
    colour_stage(block(2, 6), geometry, held, marks)
    collide_stage(block(3, 4), geometry, held, solids, marks, walls, later)
    arrive_stage(block(4, 4), geometry, walls, later, ByRow(final))

    copies = []
    for side, row, out_row in ((0, HALO, 0), (1, SLAB, live - SUBLANES)):
        gather_tiles(final, row, pieces, side * SUBLANES)
        out_row = pl.multiple_of(out_row, SUBLANES)
        copies = copies + tile_copies(pieces, outs, side * SUBLANES, out_row, sems.at[side])
    for copy in copies:
        copy.start()
    for copy in copies:
        copy.wait()


def run_outer(info, whole, arrived, passed, slabs, outs):
    flat_count = outs[0].shape[1]
    shapes = [jax.ShapeDtypeStruct(array.shape, jnp.float32) for array in (*outs, *slabs)]
    slabs = [pltpu.with_memory_space_constraint(slab, pltpu.VMEM) for slab in slabs]
    aliases = {4 + number: 4 + number for number in range(6)}
    aliases.update({10 + number: number for number in range(4)})
    return pl.pallas_call(
        outer_kernel,
        out_shape=shapes,
        in_specs=[SMEM] + [VMEM] * 9 + [ANY] * 4,
        out_specs=[ANY] * 4 + [VMEM] * 6,
        scratch_shapes=[
            scratch_of(by_row(2 * SLAB, PLACES)),
            scratch_of(by_row(2 * SLAB, 4)),
            scratch_of(by_row(4, 3)),
            pieces_of(2 * SUBLANES, flat_count),
            pltpu.SemaphoreType.DMA((2, 4)),
        ],
        input_output_aliases=aliases,
        compiler_params=pltpu.CompilerParams(vmem_limit_bytes=24 * 1024 * 1024),
        name="outer",
    )(info, whole, arrived, passed, *slabs, *outs)


def body(density, momentum, stress, red_density, solid, widths):
    tiles_count = lax.axis_size("tiles")
    arrays = (density, momentum, stress, red_density, solid)
    info, raw, raw_solid, packet, mine = load_inputs(arrays, widths, tiles_count)
    info = pltpu.with_memory_space_constraint(info, pltpu.SMEM)
    swap = [(0, 1), (1, 0)]
    packet = lax.ppermute(packet, "sub", swap)
    spread = spread_rows(raw, raw_solid)
    ends = join_ends(mine, packet, spread)
    route = [(2 * k, 2 * k + 2) for k in range(tiles_count - 1)]
    route = route + [(2 * k + 3, 2 * k + 1) for k in range(tiles_count - 1)]
    arrived = lax.ppermute(ends, ("tiles", "sub"), route)
    whole = put_beside(info, spread, packet)
    moved, reds, earlier, *slabs = run_first(info, whole)
    arrived = follow(arrived, slabs[-1])
    passed = lax.ppermute(arrived, "sub", swap)
    outs = run_second(info, (moved, reds), earlier, arrived, arrays)
    return tuple(run_outer(info, whole, arrived, passed, slabs, outs)[:4])


def solution(mesh):
    in_specs = (
        P(("groups", "tiles"), "sub"),
        P(None, ("groups", "tiles"), "sub"),
        P(None, ("groups", "tiles"), "sub"),
        P(("groups", "tiles"), "sub"),
        P(("groups", "tiles"), "sub"),
        P("groups"),
    )
    out_specs = (
        P(("groups", "tiles"), "sub"),
        P(None, ("groups", "tiles"), "sub"),
        P(None, ("groups", "tiles"), "sub"),
        P(("groups", "tiles"), "sub"),
    )
    return jax.shard_map(body, mesh=mesh, in_specs=in_specs, out_specs=out_specs, check_vma=False)
```

profile of v0, /device:TPU:0, one launch (start us, length us, event | category | flops | bytes accessed | tf_op | source)
XLA Modules:
  0.0 19.6 jit_solution(12411757689045284683)
XLA Ops:
  0.6 1.6 %load.1 = (s32[4]{0:T(128)S(4)}, f32[11,48,768]{2,1,0:T(8,128)S(1)}, s32[48,768]{1,0:T(8,128)S(1)}, f32[512,128]{1,0:T(8,128)S(1)}, f32[224,128]{1,0:T(8,128)S(1)}) custom-call(f32[48,768]{1,0:T(8,128)} %density.1, f32[3,48,768]{2,1,0:T(8,128)} %momentum.1, f32[6,48,768]{2,1,0:T(8,128)} %stress.1, f32[48,768]{1,0:T(8,128)} %red.1, s32[48,768]{1,0:T(8,128)} %solid.1, ...), custom_call_target="tpu_custom_call" | custom-call | tf_op jit(solution)/shard_map/load/pallas_call | solution.py:556
  2.3 0.5 %collective-permute-start = (f32[512,128]{1,0:T(8,128)S(1)}, f32[512,128]{1,0:T(8,128)S(1)}, u32[]{:S(2)}, u32[]{:S(2)}) collective-permute-start(f32[512,128]{1,0:T(8,128)S(1)} %get-tuple-element.29), channel_id=1, source_target_pairs={{0,1},{1,0},{2,3},{3,2},{4,5},{5,4},{6,7},{7,6},{8,9},{9,8},{10,11... | collective-permute-start | bytes 786440 | tf_op jit(solution)/shard_map/ppermute | solution.py:933
  2.8 0.3 %spread.1 = f32[48,104,128]{2,1,0:T(8,128)S(1)} custom-call(f32[11,48,768]{2,1,0:T(8,128)S(1)} %get-tuple-element.27.raw, s32[48,768]{1,0:T(8,128)S(1)} %get-tuple-element.28.raw_solid), custom_call_target="tpu_custom_call" | custom-call | flops 1000000 | bytes 4000000 | tf_op jit(solution)/shard_map/spread/pallas_call | solution.py:586
  3.1 0.9 %collective-permute-done.packet = f32[512,128]{1,0:T(8,128)S(1)} collective-permute-done((f32[512,128]{1,0:T(8,128)S(1)}, f32[512,128]{1,0:T(8,128)S(1)}, u32[]{:S(2)}, u32[]{:S(2)}) %collective-permute-start) | collective-permute-done | bytes 262176 | tf_op jit(solution)/shard_map/ppermute | solution.py:933
  4.0 4.8 %collective-permute-start.1 = (f32[448,128]{1,0:T(8,128)S(1)}, f32[448,128]{1,0:T(8,128)S(1)}, u32[]{:S(2)}, u32[]{:S(2)}) collective-permute-start(f32[448,128]{1,0:T(8,128)S(1)} %join.1), channel_id=1, source_target_pairs={{0,2},{2,4},{4,6},{6,8},{8,10},{10,12},{12,14},{3,1},{5,3},{7,5},{... | collective-permute-start | bytes 688136 | tf_op jit(solution)/shard_map/ppermute | solution.py:938
  8.8 0.1 beside.1.whole
  8.9 6.7 %first.1 = (f32[48,160,128]{2,1,0:T(8,128)S(1)}, f32[48,40,128]{2,1,0:T(8,128)S(1)}, f32[48,88,128]{2,1,0:T(8,128)S(1)}, f32[24,160,128]{2,1,0:T(8,128)S(1)}, f3...) custom-call(s32[4]{0:T(128)S(4)} %get-tuple-element.26.info, ...), custom_call_target="tpu_custom_call" | custom-call | flops 20000000 | bytes 8000000 | tf_op jit(solution)/shard_map/first/pallas_call | solution.py:790
  15.6 0.0 collective-permute-done.1.ends
  15.6 0.1 collective-permute-start.2
  15.7 1.5 %second.1 = (f32[48,768]{1,0:T(8,128)}, f32[3,48,768]{2,1,0:T(8,128)}, f32[6,48,768]{2,1,0:T(8,128)}, f32[48,768]{1,0:T(8,128)}) custom-call(s32[4]{0:T(128)S(4)} %get-tuple-element.26.info, f32[48,160,128]{2,1,0:T(8,128)S(1)} %get-tuple-element.37.moved, f32[48,40,128]{2,1,0:T(8,128)S(1)} %get-tuple-element.38.reds, ...), custom_call_target="tpu_custom_call" | custom-call | flops 20000000 | bytes 8000000 | tf_op jit(solution)/shard_map/second/pallas_call | solution.py:804
  17.2 0.0 collective-permute-done.2.passed
  17.3 2.4 %outer.1 = (f32[48,768]{1,0:T(8,128)}, f32[3,48,768]{2,1,0:T(8,128)}, f32[6,48,768]{2,1,0:T(8,128)}, f32[48,768]{1,0:T(8,128)}, f32[24,160,128]{2,1,0:T(8,128)S(...) custom-call(s32[4]{0:T(128)S(4)} %get-tuple-element.26.info, ...), custom_call_target="tpu_custom_call", output_to_operand_aliasing={{4}: (4, {}), {5}: (5, {}), {6}: (6, {}), {7}: (7, {}), {8}... | custom-call | tf_op jit(solution)/shard_map/outer/pallas_call | solution.py:909
  (2 shorter events, 0.0 us)
Async XLA Ops:
  2.3 1.7 %collective-permute-start = (f32[512,128]{1,0:T(8,128)S(1)}, f32[512,128]{1,0:T(8,128)S(1)}, u32[]{:S(2)}, u32[]{:S(2)}) collective-permute-start(f32[512,128]{1,0:T(8,128)S(1)} %get-tuple-element.29), channel_id=1, source_target_pairs={{0,1},{1,0},{2,3},{3,2},{4,5},{5,4},{6,7},{7,6},{8,9},{9,8},{10,11... | collective-permute-start | bytes 786440 | tf_op jit(solution)/shard_map/ppermute | solution.py:933
  4.0 11.7 %collective-permute-start.1 = (f32[448,128]{1,0:T(8,128)S(1)}, f32[448,128]{1,0:T(8,128)S(1)}, u32[]{:S(2)}, u32[]{:S(2)}) collective-permute-start(f32[448,128]{1,0:T(8,128)S(1)} %join.1), channel_id=1, source_target_pairs={{0,2},{2,4},{4,6},{6,8},{8,10},{10,12},{12,14},{3,1},{5,3},{7,5},{... | collective-permute-start | bytes 688136 | tf_op jit(solution)/shard_map/ppermute | solution.py:938
  15.6 1.6 %collective-permute-start.2 = (f32[448,128]{1,0:T(8,128)S(1)}, f32[448,128]{1,0:T(8,128)S(1)}, u32[]{:S(2)}, u32[]{:S(2)}) collective-permute-start(f32[448,128]{1,0:T(8,128)S(1)} %follow.1.arrived), channel_id=1, source_target_pairs={{0,1},{1,0},{2,3},{3,2},{4,5},{5,4},{6,7},{7,6},{8,9},{9,8},{10,11... | collective-permute-start | bytes 688136 | tf_op jit(solution)/shard_map/ppermute | solution.py:942
where the time goes:
time: 19.4 us; the launch traced here: 19.6 us
  Pallas kernels  12.6 us (65%)
  starting transfers between devices  5.39 us (28%)
  waiting for transfers between devices  0.86 us (4%)
  between operations  0.71 us (4%)
    pallas_call x1, Pallas kernels, run_first(): pl.pallas_call(first_kernel, out_shape=shapes + slabs, in_specs=[SMEM, VM...  6.73 us
    ppermute x1, starting transfers between devices, body(): arrived = lax.ppermute(ends, ('tiles', 'sub'), route)  4.81 us
    pallas_call x1, Pallas kernels, run_outer(): pl.pallas_call(outer_kernel, out_shape=shapes, in_specs=[SMEM] + [VMEM] *...  2.36 us
    pallas_call x1, Pallas kernels, load_inputs(): pl.pallas_call(functools.partial(load_kernel, tiles_count), out_shape=[pl...  1.61 us
    pallas_call x1, Pallas kernels, run_second(): pl.pallas_call(second_kernel, out_shape=[jax.ShapeDtypeStruct(array.shape...  1.51 us
    ppermute x1, waiting for transfers between devices, body(): packet = lax.ppermute(packet, 'sub', swap)  0.86 us
    ppermute x1, starting transfers between devices, body(): packet = lax.ppermute(packet, 'sub', swap)  0.52 us
  transfers between devices with their start and end apart: 3, of which 1 were waited for; matrix products, arithmetic and copies ran while one was open for 0% of the time, Pallas kernels for 44%

commit v1 on v0

--- a/solution.py
+++ b/solution.py
@@ -32,11 +32,12 @@
 ORDER = (0, 1, 2, 3, 10, 11, 4, 5, 6, 7, 8, 9)
 PAIRS = PLANES // 2
 PLACES = PLANES + 1
-SPLIT = 4
+SPLIT = 5
 KEPT = 2
+OUT_COPIES = 5
 COLOUR_BLOCK = (16, 1)
 COLLIDE_BLOCK = (8, 1)
-ARRIVE_BLOCK = (8, 1)
+ARRIVE_BLOCK = (16, 1)
 VMEM = pl.BlockSpec(memory_space=pltpu.VMEM)
 SMEM = pl.BlockSpec(memory_space=pltpu.SMEM)
 ANY = pl.BlockSpec(memory_space=pl.ANY)
@@ -478,15 +479,12 @@
 ):
     row_count, flat_count = raw_solid.shape
     own_tiles = flat_count // LANES
-    copies = [
-        pltpu.make_async_copy(widths, held_widths, sems.at[0]),
-        pltpu.make_async_copy(density, raw.at[0], sems.at[1]),
-        pltpu.make_async_copy(momentum, raw.at[pl.ds(1, 3)], sems.at[2]),
-        pltpu.make_async_copy(red, raw.at[10], sems.at[3]),
-        pltpu.make_async_copy(solid, raw_solid, sems.at[4]),
-        pltpu.make_async_copy(stress.at[pl.ds(0, 3)], raw.at[pl.ds(4, 3)], sems.at[5]),
-        pltpu.make_async_copy(stress.at[pl.ds(3, 3)], raw.at[pl.ds(7, 3)], sems.at[6]),
-    ]
+    planes = [density] + [momentum.at[axis] for axis in range(3)]
+    planes = planes + [stress.at[part] for part in range(6)] + [red, solid]
+    copies = [pltpu.make_async_copy(widths, held_widths, sems.at[PLANES])]
+    for index in ORDER:
+        target = raw_solid if index == FIELDS else raw.at[index]
+        copies.append(pltpu.make_async_copy(planes[index], target, sems.at[index]))
     for copy in copies:
         copy.start()
     tiles_index, sub_index = lax.axis_index("tiles"), lax.axis_index("sub")
@@ -533,13 +531,11 @@
                 place = (group * (GROUP - 1) + number) * SUBLANES
                 target[pl.ds(place, SUBLANES), :] = block
 
-    place = 0
-    for copy, count in zip(copies[1:], (1, 3, 1, 1, 3, 3)):
+    for before, (copy, index) in enumerate(zip(copies[1:], ORDER)):
+        place = before + 1
         copy.wait()
-        before, place = place, place + count
-        for index in ORDER[before:place]:
-            for target, row in ((first_tile, 0), (last_tile, near_last)):
-                spread_tile(raw, raw_solid, index, row, target, 0)
+        for target, row in ((first_tile, 0), (last_tile, near_last)):
+            spread_tile(raw, raw_solid, index, row, target, 0)
         for pair in range(before // 2, place // 2):
             pack_edges(pair)
         for group in range(before * FULL // GROUP, place * FULL // GROUP):
@@ -568,7 +564,7 @@
             pltpu.VMEM((SUBLANES, PLACES * SUBLANES, LANES), jnp.float32),
             pltpu.VMEM((SUBLANES, PLACES * SUBLANES, LANES), jnp.float32),
             pltpu.SMEM(widths.shape, jnp.int32),
-            pltpu.SemaphoreType.DMA((7,)),
+            pltpu.SemaphoreType.DMA((PLANES + 1,)),
         ],
         compiler_params=pltpu.CompilerParams(vmem_limit_bytes=16 * 1024 * 1024),
         name="load",
@@ -661,7 +657,8 @@
     parts = (
         (pieces.at[0, held], outs[0].at[rows]),
         (pieces.at[pl.ds(1, 3), held], outs[1].at[:, rows]),
-        (pieces.at[pl.ds(4, 6), held], outs[2].at[:, rows]),
+        (pieces.at[pl.ds(4, 3), held], outs[2].at[pl.ds(0, 3), rows]),
+        (pieces.at[pl.ds(7, 3), held], outs[2].at[pl.ds(3, 3), rows]),
         (pieces.at[10, held], outs[3].at[rows]),
     )
     return [
@@ -811,7 +808,7 @@
             scratch_of(by_row(4, 3)),
             pieces_of(row_count, flat_count),
             pieces_of(SUBLANES, flat_count),
-            pltpu.SemaphoreType.DMA((row_count // SUBLANES, 4)),
+            pltpu.SemaphoreType.DMA((row_count // SUBLANES, OUT_COPIES)),
         ],
         compiler_params=pltpu.CompilerParams(vmem_limit_bytes=24 * 1024 * 1024),
         cost_estimate=pl.CostEstimate(flops=20_000_000, bytes_accessed=8_000_000, transcendentals=0),
@@ -916,7 +913,7 @@
             scratch_of(by_row(2 * SLAB, 4)),
             scratch_of(by_row(4, 3)),
             pieces_of(2 * SUBLANES, flat_count),
-            pltpu.SemaphoreType.DMA((2, 4)),
+            pltpu.SemaphoreType.DMA((2, OUT_COPIES)),
         ],
         input_output_aliases=aliases,
         compiler_params=pltpu.CompilerParams(vmem_limit_bytes=24 * 1024 * 1024),

time: 19.4 us -> 19.1 us (0.985)
  the two profiles are of different devices: /device:TPU:0 before, /device:TPU:27 now
where the time goes in v1:
time: 19.1 us; the launch traced here: 18.9 us
  Pallas kernels  12.8 us (67%)
  starting transfers between devices  4.61 us (24%)
  waiting for transfers between devices  0.86 us (5%)
  between operations  0.7 us (4%)
    pallas_call x1, Pallas kernels, run_first(): pl.pallas_call(first_kernel, out_shape=shapes + slabs, in_specs=[SMEM, VM...  6.93 us
    ppermute x1, starting transfers between devices, body(): arrived = lax.ppermute(ends, ('tiles', 'sub'), route)  3.03 us
    pallas_call x1, Pallas kernels, run_outer(): pl.pallas_call(outer_kernel, out_shape=shapes, in_specs=[SMEM] + [VMEM] *...  2.37 us
    pallas_call x1, Pallas kernels, load_inputs(): pl.pallas_call(functools.partial(load_kernel, tiles_count), out_shape=[pl...  1.73 us
    pallas_call x1, Pallas kernels, run_second(): pl.pallas_call(second_kernel, out_shape=[jax.ShapeDtypeStruct(array.shape...  1.29 us
    ppermute x1, waiting for transfers between devices, body(): packet = lax.ppermute(packet, 'sub', swap)  0.86 us
    ppermute x1, starting transfers between devices, body(): passed = lax.ppermute(arrived, 'sub', swap)  0.83 us
    ppermute x1, starting transfers between devices, body(): packet = lax.ppermute(packet, 'sub', swap)  0.74 us
  transfers between devices with their start and end apart: 3, of which 1 were waited for; matrix products, arithmetic and copies ran while one was open for 0% of the time, Pallas kernels for 46%

profile of v1, /device:TPU:27, one launch (start us, length us, event | category | flops | bytes accessed | tf_op | source)
XLA Modules:
  0.0 18.9 jit_solution(1442327710121780590)
XLA Ops:
  0.6 1.7 %load.1 = (s32[4]{0:T(128)S(4)}, f32[11,48,768]{2,1,0:T(8,128)S(1)}, s32[48,768]{1,0:T(8,128)S(1)}, f32[512,128]{1,0:T(8,128)S(1)}, f32[224,128]{1,0:T(8,128)S(1)}) custom-call(f32[48,768]{1,0:T(8,128)} %density.1, f32[3,48,768]{2,1,0:T(8,128)} %momentum.1, f32[6,48,768]{2,1,0:T(8,128)} %stress.1, f32[48,768]{1,0:T(8,128)} %red.1, s32[48,768]{1,0:T(8,128)} %solid.1, ...), custom_call_target="tpu_custom_call" | custom-call | tf_op jit(solution)/shard_map/load/pallas_call | solution.py:552
  2.4 0.7 %collective-permute-start = (f32[512,128]{1,0:T(8,128)S(1)}, f32[512,128]{1,0:T(8,128)S(1)}, u32[]{:S(2)}, u32[]{:S(2)}) collective-permute-start(f32[512,128]{1,0:T(8,128)S(1)} %get-tuple-element.29), channel_id=1, source_target_pairs={{0,1},{1,0},{2,3},{3,2},{4,5},{5,4},{6,7},{7,6},{8,9},{9,8},{10,11... | collective-permute-start | bytes 786440 | tf_op jit(solution)/shard_map/ppermute | solution.py:930
  3.1 0.3 %spread.1 = f32[48,104,128]{2,1,0:T(8,128)S(1)} custom-call(f32[11,48,768]{2,1,0:T(8,128)S(1)} %get-tuple-element.27.raw, s32[48,768]{1,0:T(8,128)S(1)} %get-tuple-element.28.raw_solid), custom_call_target="tpu_custom_call" | custom-call | flops 1000000 | bytes 4000000 | tf_op jit(solution)/shard_map/spread/pallas_call | solution.py:582
  3.4 0.9 %collective-permute-done.packet = f32[512,128]{1,0:T(8,128)S(1)} collective-permute-done((f32[512,128]{1,0:T(8,128)S(1)}, f32[512,128]{1,0:T(8,128)S(1)}, u32[]{:S(2)}, u32[]{:S(2)}) %collective-permute-start) | collective-permute-done | bytes 262176 | tf_op jit(solution)/shard_map/ppermute | solution.py:930
  4.3 3.0 %collective-permute-start.1 = (f32[448,128]{1,0:T(8,128)S(1)}, f32[448,128]{1,0:T(8,128)S(1)}, u32[]{:S(2)}, u32[]{:S(2)}) collective-permute-start(f32[448,128]{1,0:T(8,128)S(1)} %join.1), channel_id=1, source_target_pairs={{0,2},{2,4},{4,6},{6,8},{8,10},{10,12},{12,14},{3,1},{5,3},{7,5},{... | collective-permute-start | bytes 688136 | tf_op jit(solution)/shard_map/ppermute | solution.py:935
  7.3 0.1 beside.1.whole
  7.5 6.9 %first.1 = (f32[48,160,128]{2,1,0:T(8,128)S(1)}, f32[48,40,128]{2,1,0:T(8,128)S(1)}, f32[48,88,128]{2,1,0:T(8,128)S(1)}, f32[24,160,128]{2,1,0:T(8,128)S(1)}, f3...) custom-call(s32[4]{0:T(128)S(4)} %get-tuple-element.26.info, ...), custom_call_target="tpu_custom_call" | custom-call | flops 20000000 | bytes 8000000 | tf_op jit(solution)/shard_map/first/pallas_call | solution.py:787
  14.4 0.0 collective-permute-done.1.ends
  14.4 0.8 %collective-permute-start.2 = (f32[448,128]{1,0:T(8,128)S(1)}, f32[448,128]{1,0:T(8,128)S(1)}, u32[]{:S(2)}, u32[]{:S(2)}) collective-permute-start(f32[448,128]{1,0:T(8,128)S(1)} %follow.1.arrived), channel_id=1, source_target_pairs={{0,1},{1,0},{2,3},{3,2},{4,5},{5,4},{6,7},{7,6},{8,9},{9,8},{10,11... | collective-permute-start | bytes 688136 | tf_op jit(solution)/shard_map/ppermute | solution.py:939
  15.2 1.3 %second.1 = (f32[48,768]{1,0:T(8,128)}, f32[3,48,768]{2,1,0:T(8,128)}, f32[6,48,768]{2,1,0:T(8,128)}, f32[48,768]{1,0:T(8,128)}) custom-call(s32[4]{0:T(128)S(4)} %get-tuple-element.26.info, f32[48,160,128]{2,1,0:T(8,128)S(1)} %get-tuple-element.37.moved, f32[48,40,128]{2,1,0:T(8,128)S(1)} %get-tuple-element.38.reds, ...), custom_call_target="tpu_custom_call" | custom-call | flops 20000000 | bytes 8000000 | tf_op jit(solution)/shard_map/second/pallas_call | solution.py:801
  16.5 0.0 collective-permute-done.2.passed
  16.6 2.4 %outer.1 = (f32[48,768]{1,0:T(8,128)}, f32[3,48,768]{2,1,0:T(8,128)}, f32[6,48,768]{2,1,0:T(8,128)}, f32[48,768]{1,0:T(8,128)}, f32[24,160,128]{2,1,0:T(8,128)S(...) custom-call(s32[4]{0:T(128)S(4)} %get-tuple-element.26.info, ...), custom_call_target="tpu_custom_call", output_to_operand_aliasing={{4}: (4, {}), {5}: (5, {}), {6}: (6, {}), {7}: (7, {}), {8}... | custom-call | tf_op jit(solution)/shard_map/outer/pallas_call | solution.py:906
  (2 shorter events, 0.0 us)
Async XLA Ops:
  2.4 1.9 %collective-permute-start = (f32[512,128]{1,0:T(8,128)S(1)}, f32[512,128]{1,0:T(8,128)S(1)}, u32[]{:S(2)}, u32[]{:S(2)}) collective-permute-start(f32[512,128]{1,0:T(8,128)S(1)} %get-tuple-element.29), channel_id=1, source_target_pairs={{0,1},{1,0},{2,3},{3,2},{4,5},{5,4},{6,7},{7,6},{8,9},{9,8},{10,11... | collective-permute-start | bytes 786440 | tf_op jit(solution)/shard_map/ppermute | solution.py:930
  4.3 10.1 %collective-permute-start.1 = (f32[448,128]{1,0:T(8,128)S(1)}, f32[448,128]{1,0:T(8,128)S(1)}, u32[]{:S(2)}, u32[]{:S(2)}) collective-permute-start(f32[448,128]{1,0:T(8,128)S(1)} %join.1), channel_id=1, source_target_pairs={{0,2},{2,4},{4,6},{6,8},{8,10},{10,12},{12,14},{3,1},{5,3},{7,5},{... | collective-permute-start | bytes 688136 | tf_op jit(solution)/shard_map/ppermute | solution.py:935
  14.4 2.1 %collective-permute-start.2 = (f32[448,128]{1,0:T(8,128)S(1)}, f32[448,128]{1,0:T(8,128)S(1)}, u32[]{:S(2)}, u32[]{:S(2)}) collective-permute-start(f32[448,128]{1,0:T(8,128)S(1)} %follow.1.arrived), channel_id=1, source_target_pairs={{0,1},{1,0},{2,3},{3,2},{4,5},{5,4},{6,7},{7,6},{8,9},{9,8},{10,11... | collective-permute-start | bytes 688136 | tf_op jit(solution)/shard_map/ppermute | solution.py:939

commit v2 on v0

--- a/solution.py
+++ b/solution.py
@@ -32,11 +32,11 @@
 ORDER = (0, 1, 2, 3, 10, 11, 4, 5, 6, 7, 8, 9)
 PAIRS = PLANES // 2
 PLACES = PLANES + 1
-SPLIT = 4
 KEPT = 2
+OUT_COPIES = 5
 COLOUR_BLOCK = (16, 1)
-COLLIDE_BLOCK = (8, 1)
-ARRIVE_BLOCK = (8, 1)
+COLLIDE_BLOCK = (16, 1)
+ARRIVE_BLOCK = (16, 1)
 VMEM = pl.BlockSpec(memory_space=pltpu.VMEM)
 SMEM = pl.BlockSpec(memory_space=pltpu.SMEM)
 ANY = pl.BlockSpec(memory_space=pl.ANY)
@@ -656,12 +656,13 @@
         block, geometry, before, whole, colours, walls, state))
 
 
-def tile_copies(pieces, outs, held_row, out_row, sems):
-    held, rows = pl.ds(held_row, SUBLANES), pl.ds(out_row, SUBLANES)
+def row_copies(pieces, outs, held_row, out_row, count, sems):
+    held, rows = pl.ds(held_row, count), pl.ds(out_row, count)
     parts = (
         (pieces.at[0, held], outs[0].at[rows]),
         (pieces.at[pl.ds(1, 3), held], outs[1].at[:, rows]),
-        (pieces.at[pl.ds(4, 6), held], outs[2].at[:, rows]),
+        (pieces.at[pl.ds(4, 3), held], outs[2].at[pl.ds(0, 3), rows]),
+        (pieces.at[pl.ds(7, 3), held], outs[2].at[pl.ds(3, 3), rows]),
         (pieces.at[10, held], outs[3].at[rows]),
     )
     return [
@@ -684,9 +685,9 @@
 
 
 def first_kernel(
-    info, whole, moved_later, reds_later, final,
+    info, whole, final,
     moved_slab, reds_slab, fields_slab, moved_later_slab, reds_later_slab, final_slab,
-    colours, walls, moved, reds, fields,
+    colours, walls, moved, reds, fields, moved_later, reds_later,
 ):
     state, later = (ByRow(moved), ByRow(reds)), (ByRow(moved_later), ByRow(reds_later))
     geometry = Geometry(info, OWN_TILES)
@@ -705,72 +706,41 @@
     rim = Block(geometry, [(row, row, RIM) for _, row in edges], True, [at for at, _ in edges])
     arrive_stage(rim, geometry, walls, later, ByRow(final_slab))
 
-    def arrive_tile(tile, carry):
-        row = tile * SUBLANES
-        block = Block(geometry, [(row, row, SUBLANES)], inner=True)
+    def finish(index, carry):
+        row = SUBLANES + index * TILE
+        block = Block(geometry, [(row, row, TILE)], inner=True)
         arrive_stage(block, geometry, walls, later, ByRow(final))
         return carry
 
-    lax.fori_loop(1, jnp.minimum(SPLIT, live // SUBLANES - 1), arrive_tile, 0)
-
-
-def second_kernel(
-    info, moved, reds, earlier, arrived, density_out, momentum_out, stress_out, red_out,
-    final, walls, pieces, zeros, sems,
-):
+    lax.fori_loop(0, live // TILE - 1, finish, 0)
+
+
+def second_kernel(info, final, arrived, density_out, momentum_out, stress_out, red_out, pieces, sems):
     outs = (density_out, momentum_out, stress_out, red_out)
-    row_tiles = density_out.shape[0] // SUBLANES
-    state = (ByRow(moved), ByRow(reds))
-    geometry = Geometry(info, OWN_TILES)
-    live = geometry.live
-    last = live // SUBLANES - 1
-    fill_wall_table(walls, geometry)
-
-    def copies_of(tile):
-        row = pl.multiple_of(tile * SUBLANES, SUBLANES)
-        return tile_copies(pieces, outs, row, row, sems.at[tile])
-
-    def send_out(tile, source):
-        row = pl.multiple_of(tile * SUBLANES, SUBLANES)
-        gather_tiles(source, row, pieces, row)
-        for copy in copies_of(tile):
+    live = info[0]
+    copies = []
+    for number, (least, inner_row, dead_row) in enumerate(
+        ((2 * TILE, SUBLANES, TILE), (3 * TILE, SUBLANES + TILE, 2 * TILE))
+    ):
+        held_row = number * TILE
+
+        @pl.when(live >= least)
+        def _():
+            for extra in range(0, TILE, SUBLANES):
+                gather_tiles(final, inner_row + extra, pieces, held_row + extra)
+
+        @pl.when(live < least)
+        def _():
+            zeros = jnp.zeros((FIELDS, TILE, pieces.shape[2]), jnp.float32)
+            pieces[:, pl.ds(held_row, TILE), :] = zeros
+
+        row = pl.multiple_of(jnp.where(live >= least, inner_row, dead_row), SUBLANES)
+        started = row_copies(pieces, outs, held_row, row, TILE, sems.at[number])
+        for copy in started:
             copy.start()
-
-    def pass_on(tile, carry):
-        send_out(tile, earlier)
-        return carry
-
-    def finish(tile, carry):
-        row = tile * SUBLANES
-        block = Block(geometry, [(row, row, SUBLANES)], inner=True)
-        arrive_stage(block, geometry, walls, state, ByRow(final))
-        send_out(tile, final)
-        return carry
-
-    def settle(tile, carry):
-        for copy in copies_of(tile):
-            copy.wait()
-        return carry
-
-    lax.fori_loop(1, jnp.minimum(SPLIT, last), pass_on, 0)
-    zeros[...] = jnp.zeros(zeros.shape, zeros.dtype)
-    dead = {}
-    for tile in range(row_tiles):
-        dead[tile] = tile_copies(zeros, outs, 0, tile * SUBLANES, sems.at[tile])
-
-        @pl.when(tile * SUBLANES >= live)
-        def _():
-            for copy in dead[tile]:
-                copy.start()
-
-    lax.fori_loop(SPLIT, last, finish, 0)
-    lax.fori_loop(1, last, settle, 0)
-    for tile in range(row_tiles):
-
-        @pl.when(tile * SUBLANES >= live)
-        def _():
-            for copy in dead[tile]:
-                copy.wait()
+        copies = copies + started
+    for copy in copies:
+        copy.wait()
 
 
 def scratch_of(shape):
@@ -783,40 +753,37 @@
 
 def run_first(info, whole):
     rows = whole.shape[0]
-    shapes = [by_row(rows, count) for count in (HELD, REDS, FIELDS)]
     slabs = [by_row(2 * SLAB, count) for count in (HELD, REDS, FIELDS, HELD, REDS, FIELDS)]
     scratch = [by_row(rows, 4), by_row(4, 3)]
-    scratch = scratch + [by_row(rows, count) for count in (HELD, REDS, FIELDS)]
+    scratch = scratch + [by_row(rows, count) for count in (HELD, REDS, FIELDS, HELD, REDS)]
     return pl.pallas_call(
         first_kernel,
-        out_shape=shapes + slabs,
+        out_shape=[by_row(rows, FIELDS)] + slabs,
         in_specs=[SMEM, VMEM],
-        out_specs=[VMEM] * 9,
+        out_specs=[VMEM] * 7,
         scratch_shapes=[scratch_of(shape) for shape in scratch],
-        compiler_params=pltpu.CompilerParams(vmem_limit_bytes=24 * 1024 * 1024),
-        cost_estimate=pl.CostEstimate(flops=20_000_000, bytes_accessed=8_000_000, transcendentals=0),
+        compiler_params=pltpu.CompilerParams(vmem_limit_bytes=32 * 1024 * 1024),
+        cost_estimate=pl.CostEstimate(flops=40_000_000, bytes_accessed=8_000_000, transcendentals=0),
         name="first",
     )(info, whole)
 
 
-def run_second(info, state, earlier, arrived, arrays):
+def run_second(info, final, arrived, arrays):
     row_count, flat_count = arrays[0].shape
+    assert row_count == 3 * TILE
     return pl.pallas_call(
         second_kernel,
         out_shape=[jax.ShapeDtypeStruct(array.shape, jnp.float32) for array in arrays[:4]],
-        in_specs=[SMEM] + [VMEM] * 3 + [ANY],
+        in_specs=[SMEM, VMEM, ANY],
         out_specs=[ANY] * 4,
         scratch_shapes=[
-            scratch_of(by_row(row_count, FIELDS)),
-            scratch_of(by_row(4, 3)),
-            pieces_of(row_count, flat_count),
-            pieces_of(SUBLANES, flat_count),
-            pltpu.SemaphoreType.DMA((row_count // SUBLANES, 4)),
+            pieces_of(2 * TILE, flat_count),
+            pltpu.SemaphoreType.DMA((2, OUT_COPIES)),
         ],
-        compiler_params=pltpu.CompilerParams(vmem_limit_bytes=24 * 1024 * 1024),
+        compiler_params=pltpu.CompilerParams(vmem_limit_bytes=16 * 1024 * 1024),
         cost_estimate=pl.CostEstimate(flops=20_000_000, bytes_accessed=8_000_000, transcendentals=0),
         name="second",
-    )(info, *state, earlier, arrived)
+    )(info, final, arrived)
 
 
 def follow_kernel(ends, kept, out):
@@ -893,7 +860,9 @@
     for side, row, out_row in ((0, HALO, 0), (1, SLAB, live - SUBLANES)):
         gather_tiles(final, row, pieces, side * SUBLANES)
         out_row = pl.multiple_of(out_row, SUBLANES)
-        copies = copies + tile_copies(pieces, outs, side * SUBLANES, out_row, sems.at[side])
+        copies = copies + row_copies(
+            pieces, outs, side * SUBLANES, out_row, SUBLANES, sems.at[side]
+        )
     for copy in copies:
         copy.start()
     for copy in copies:
@@ -916,7 +885,7 @@
             scratch_of(by_row(2 * SLAB, 4)),
             scratch_of(by_row(4, 3)),
             pieces_of(2 * SUBLANES, flat_count),
-            pltpu.SemaphoreType.DMA((2, 4)),
+            pltpu.SemaphoreType.DMA((2, OUT_COPIES)),
         ],
         input_output_aliases=aliases,
         compiler_params=pltpu.CompilerParams(vmem_limit_bytes=24 * 1024 * 1024),
@@ -937,10 +906,10 @@
     route = route + [(2 * k + 3, 2 * k + 1) for k in range(tiles_count - 1)]
     arrived = lax.ppermute(ends, ("tiles", "sub"), route)
     whole = put_beside(info, spread, packet)
-    moved, reds, earlier, *slabs = run_first(info, whole)
+    final, *slabs = run_first(info, whole)
     arrived = follow(arrived, slabs[-1])
     passed = lax.ppermute(arrived, "sub", swap)
-    outs = run_second(info, (moved, reds), earlier, arrived, arrays)
+    outs = run_second(info, final, arrived, arrays)
     return tuple(run_outer(info, whole, arrived, passed, slabs, outs)[:4])
 
 

time: 19.4 us -> 19.2 us (0.990)
  Pallas kernels: 12.6 us -> 12.2 us
  waiting for transfers between devices: 0.86 us -> 1.16 us
    pallas_call x1, Pallas kernels: 1.51 us -> 1.16 us  [run_second(): pl.pallas_call(second_kernel, out_shape=[jax.ShapeDtypeStruct(array.shape...]
    ppermute x1, waiting for transfers between devices: 0.01 us -> 0.3 us  [body(): passed = lax.ppermute(arrived, 'sub', swap)]
  transfers between devices with their start and end apart: 3 -> 3, of which waited for: 1 -> 2; matrix products, arithmetic and copies ran while one was open for 0% -> 0% of each run, Pallas kernels for 44% -> 42%
where the time goes in v2:
time: 19.2 us; the launch traced here: 19.4 us
  Pallas kernels  12.2 us (64%)
  starting transfers between devices  5.39 us (28%)
  waiting for transfers between devices  1.16 us (6%)
  between operations  0.7 us (4%)
    pallas_call x1, Pallas kernels, run_first(): pl.pallas_call(first_kernel, out_shape=[by_row(rows, FIELDS)] + slabs, in...  6.6 us
    ppermute x1, starting transfers between devices, body(): arrived = lax.ppermute(ends, ('tiles', 'sub'), route)  4.81 us
    pallas_call x1, Pallas kernels, run_outer(): pl.pallas_call(outer_kernel, out_shape=shapes, in_specs=[SMEM] + [VMEM] *...  2.37 us
    pallas_call x1, Pallas kernels, load_inputs(): pl.pallas_call(functools.partial(load_kernel, tiles_count), out_shape=[pl...  1.61 us
    pallas_call x1, Pallas kernels, run_second(): pl.pallas_call(second_kernel, out_shape=[jax.ShapeDtypeStruct(array.shape...  1.16 us
    ppermute x1, waiting for transfers between devices, body(): packet = lax.ppermute(packet, 'sub', swap)  0.86 us
    ppermute x1, starting transfers between devices, body(): packet = lax.ppermute(packet, 'sub', swap)  0.52 us
  transfers between devices with their start and end apart: 3, of which 2 were waited for; matrix products, arithmetic and copies ran while one was open for 0% of the time, Pallas kernels for 42%

profile of v2, /device:TPU:0, one launch (start us, length us, event | category | flops | bytes accessed | tf_op | source)
XLA Modules:
  0.0 19.4 jit_solution(12039747750929441078)
XLA Ops:
  0.6 1.6 %load.1 = (s32[4]{0:T(128)S(4)}, f32[11,48,768]{2,1,0:T(8,128)S(1)}, s32[48,768]{1,0:T(8,128)S(1)}, f32[512,128]{1,0:T(8,128)S(1)}, f32[224,128]{1,0:T(8,128)S(1)}) custom-call(f32[48,768]{1,0:T(8,128)} %density.1, f32[3,48,768]{2,1,0:T(8,128)} %momentum.1, f32[6,48,768]{2,1,0:T(8,128)} %stress.1, f32[48,768]{1,0:T(8,128)} %red.1, s32[48,768]{1,0:T(8,128)} %solid.1, ...), custom_call_target="tpu_custom_call" | custom-call | tf_op jit(solution)/shard_map/load/pallas_call | solution.py:556
  2.3 0.5 %collective-permute-start = (f32[512,128]{1,0:T(8,128)S(1)}, f32[512,128]{1,0:T(8,128)S(1)}, u32[]{:S(2)}, u32[]{:S(2)}) collective-permute-start(f32[512,128]{1,0:T(8,128)S(1)} %get-tuple-element.27), channel_id=1, source_target_pairs={{0,1},{1,0},{2,3},{3,2},{4,5},{5,4},{6,7},{7,6},{8,9},{9,8},{10,11... | collective-permute-start | bytes 786440 | tf_op jit(solution)/shard_map/ppermute | solution.py:902
  2.8 0.3 %spread.1 = f32[48,104,128]{2,1,0:T(8,128)S(1)} custom-call(f32[11,48,768]{2,1,0:T(8,128)S(1)} %get-tuple-element.25.raw, s32[48,768]{1,0:T(8,128)S(1)} %get-tuple-element.26.raw_solid), custom_call_target="tpu_custom_call" | custom-call | flops 1000000 | bytes 4000000 | tf_op jit(solution)/shard_map/spread/pallas_call | solution.py:586
  3.1 0.9 %collective-permute-done.packet = f32[512,128]{1,0:T(8,128)S(1)} collective-permute-done((f32[512,128]{1,0:T(8,128)S(1)}, f32[512,128]{1,0:T(8,128)S(1)}, u32[]{:S(2)}, u32[]{:S(2)}) %collective-permute-start) | collective-permute-done | bytes 262176 | tf_op jit(solution)/shard_map/ppermute | solution.py:902
  4.0 4.8 %collective-permute-start.1 = (f32[448,128]{1,0:T(8,128)S(1)}, f32[448,128]{1,0:T(8,128)S(1)}, u32[]{:S(2)}, u32[]{:S(2)}) collective-permute-start(f32[448,128]{1,0:T(8,128)S(1)} %join.1), channel_id=1, source_target_pairs={{0,2},{2,4},{4,6},{6,8},{8,10},{10,12},{12,14},{3,1},{5,3},{7,5},{... | collective-permute-start | bytes 688136 | tf_op jit(solution)/shard_map/ppermute | solution.py:907
  8.8 0.1 beside.1.whole
  8.9 6.6 %first.1 = (f32[48,88,128]{2,1,0:T(8,128)S(1)}, f32[24,160,128]{2,1,0:T(8,128)S(1)}, f32[24,40,128]{2,1,0:T(8,128)S(1)}, f32[24,88,128]{2,1,0:T(8,128)S(1)}, f32...) custom-call(s32[4]{0:T(128)S(4)} %get-tuple-element.24.info, ...), custom_call_target="tpu_custom_call" | custom-call | flops 40000000 | bytes 8000000 | tf_op jit(solution)/shard_map/first/pallas_call | solution.py:759
  15.5 0.0 collective-permute-done.1.ends
  15.5 0.1 collective-permute-start.2
  15.6 1.2 %second.1 = (f32[48,768]{1,0:T(8,128)}, f32[3,48,768]{2,1,0:T(8,128)}, f32[6,48,768]{2,1,0:T(8,128)}, f32[48,768]{1,0:T(8,128)}) custom-call(s32[4]{0:T(128)S(4)} %get-tuple-element.24.info, f32[48,88,128]{2,1,0:T(8,128)S(1)} %get-tuple-element.35.final, f32[448,128]{1,0:T(8,128)S(1)} %follow.1.arrived), custom_call_target="tpu_custom_call" | custom-call | flops 20000000 | bytes 8000000 | tf_op jit(solution)/shard_map/second/pallas_call | solution.py:774
  16.8 0.3 %collective-permute-done.2.passed = f32[448,128]{1,0:T(8,128)S(1)} collective-permute-done((f32[448,128]{1,0:T(8,128)S(1)}, f32[448,128]{1,0:T(8,128)S(1)}, u32[]{:S(2)}, u32[]{:S(2)}) %collective-permute-start.2) | collective-permute-done | bytes 229408 | tf_op jit(solution)/shard_map/ppermute | solution.py:911
  17.1 2.4 %outer.1 = (f32[48,768]{1,0:T(8,128)}, f32[3,48,768]{2,1,0:T(8,128)}, f32[6,48,768]{2,1,0:T(8,128)}, f32[48,768]{1,0:T(8,128)}, f32[24,160,128]{2,1,0:T(8,128)S(...) custom-call(s32[4]{0:T(128)S(4)} %get-tuple-element.24.info, ...), custom_call_target="tpu_custom_call", output_to_operand_aliasing={{4}: (4, {}), {5}: (5, {}), {6}: (6, {}), {7}: (7, {}), {8}... | custom-call | tf_op jit(solution)/shard_map/outer/pallas_call | solution.py:878
  (2 shorter events, 0.0 us)
Async XLA Ops:
  2.3 1.7 %collective-permute-start = (f32[512,128]{1,0:T(8,128)S(1)}, f32[512,128]{1,0:T(8,128)S(1)}, u32[]{:S(2)}, u32[]{:S(2)}) collective-permute-start(f32[512,128]{1,0:T(8,128)S(1)} %get-tuple-element.27), channel_id=1, source_target_pairs={{0,1},{1,0},{2,3},{3,2},{4,5},{5,4},{6,7},{7,6},{8,9},{9,8},{10,11... | collective-permute-start | bytes 786440 | tf_op jit(solution)/shard_map/ppermute | solution.py:902
  4.0 11.5 %collective-permute-start.1 = (f32[448,128]{1,0:T(8,128)S(1)}, f32[448,128]{1,0:T(8,128)S(1)}, u32[]{:S(2)}, u32[]{:S(2)}) collective-permute-start(f32[448,128]{1,0:T(8,128)S(1)} %join.1), channel_id=1, source_target_pairs={{0,2},{2,4},{4,6},{6,8},{8,10},{10,12},{12,14},{3,1},{5,3},{7,5},{... | collective-permute-start | bytes 688136 | tf_op jit(solution)/shard_map/ppermute | solution.py:907
  15.5 1.6 %collective-permute-start.2 = (f32[448,128]{1,0:T(8,128)S(1)}, f32[448,128]{1,0:T(8,128)S(1)}, u32[]{:S(2)}, u32[]{:S(2)}) collective-permute-start(f32[448,128]{1,0:T(8,128)S(1)} %follow.1.arrived), channel_id=1, source_target_pairs={{0,1},{1,0},{2,3},{3,2},{4,5},{5,4},{6,7},{7,6},{8,9},{9,8},{10,11... | collective-permute-start | bytes 688136 | tf_op jit(solution)/shard_map/ppermute | solution.py:911

commit v3 on v2

--- a/solution.py
+++ b/solution.py
@@ -27,7 +27,8 @@
 OWN_TILES = SUBLANES - 2
 GROUP = 4
 PACKED = FULL * PLANES // GROUP * (GROUP - 1)
-END_ROWS = (PACKED + 1) * SUBLANES
+END_ROWS = PACKED * SUBLANES
+SPARE = 9
 HALF = LANES // 2
 ORDER = (0, 1, 2, 3, 10, 11, 4, 5, 6, 7, 8, 9)
 PAIRS = PLANES // 2
@@ -523,12 +524,23 @@
         last = read_row(ByRow(last_tile), index, number_last)
         return jnp.where(use_last, last, first)
 
+    def colour_of(use_last):
+        red_row, density_row = [
+            row_of(use_last, index, FULL, SUBLANES - HALO) for index in (10, 0)
+        ]
+        return 2.0 * red_row - density_row
+
     def pack_ends(group):
         for target, use_last in targets:
             blocks = []
             for number in range(group * GROUP, (group + 1) * GROUP):
                 place, extra = divmod(number, FULL)
-                blocks.append(row_of(use_last, ORDER[place], extra, SUBLANES - FULL + extra))
+                block = row_of(use_last, ORDER[place], extra, SUBLANES - FULL + extra)
+                if ORDER[place] == SPARE and extra == 0:
+                    block = jnp.where(use_last, colour_of(use_last), block)
+                if ORDER[place] == SPARE and extra == FULL - 1:
+                    block = jnp.where(use_last, block, colour_of(use_last))
+                blocks.append(block)
             for number, block in enumerate(pack_blocks(blocks)):
                 place = (group * (GROUP - 1) + number) * SUBLANES
                 target[pl.ds(place, SUBLANES), :] = block
@@ -544,11 +556,6 @@
             pack_edges(pair)
         for group in range(before * FULL // GROUP, place * FULL // GROUP):
             pack_ends(group)
-    for target, use_last in targets:
-        red_row, density_row = [
-            row_of(use_last, index, FULL, SUBLANES - HALO) for index in (10, 0)
-        ]
-        target[pl.ds(PACKED * SUBLANES, SUBLANES), :] = 2.0 * red_row - density_row
 
 
 def load_inputs(arrays, widths, tiles_count):
@@ -787,7 +794,7 @@
 
 
 def follow_kernel(ends, kept, out):
-    out[pl.ds(PACKED * SUBLANES, 1), :] = jnp.zeros((1, LANES), jnp.float32)
+    out[pl.ds(0, 1), :] = ends[pl.ds(0, 1), :]
 
 
 def follow(ends, kept):
@@ -815,11 +822,10 @@
     def ends_of(ref, half):
         blocks = []
         for group in range(FULL * PLANES // GROUP):
-            first = half * (PACKED + 1) + group * (GROUP - 1)
+            first = half * PACKED + group * (GROUP - 1)
             packed = [ref[pl.ds((first + k) * SUBLANES, SUBLANES), :] for k in range(GROUP - 1)]
             blocks = blocks + unpack_blocks(packed)
-        last = half * (PACKED + 1) + PACKED
-        return blocks + [ref[pl.ds(last * SUBLANES, SUBLANES), :]]
+        return blocks
 
     tiles = block_tiles()
     middle = (tiles >= 1) & (tiles <= OWN_TILES)
@@ -838,7 +844,10 @@
         index = ORDER[place]
         write_row(ByRow(start_fields), index, 1 + extra, below[number])
         write_row(ByRow(start_fields), index, 2 * SLAB - HALO + extra, above[number])
-    for row, colour in ((0, below[-1]), (2 * SLAB - 1, above[-1])):
+    spare = FULL * ORDER.index(SPARE)
+    ends_at = ((0, 1, below[spare]), (2 * SLAB - 1, 2 * SLAB - 2, above[spare + FULL - 1]))
+    for row, next_row, colour in ends_at:
+        write_row(ByRow(start_fields), SPARE, next_row, jnp.zeros((SUBLANES, LANES), jnp.float32))
         write_row(ByRow(start_fields), 0, row, jnp.zeros((SUBLANES, LANES), jnp.float32))
         write_row(ByRow(start_fields), 10, row, 0.5 * colour)
     for slab_row, row in slab_rows(live, HALO, FULL):

time: 19.2 us -> 19.6 us (1.021); the launches traced: 19.4 us -> 19.4 us
  no operation moved by 1% of the time
where the time goes in v3:
time: 19.6 us; the launch traced here: 19.4 us
  Pallas kernels  12.2 us (62%)
  starting transfers between devices  5.39 us (27%)
  waiting for transfers between devices  1.15 us (6%)
  between operations  0.7 us (4%)
    pallas_call x1, Pallas kernels, run_first(): pl.pallas_call(first_kernel, out_shape=[by_row(rows, FIELDS)] + slabs, in...  6.6 us
    ppermute x1, starting transfers between devices, body(): arrived = lax.ppermute(ends, ('tiles', 'sub'), route)  4.81 us
    pallas_call x1, Pallas kernels, run_outer(): pl.pallas_call(outer_kernel, out_shape=shapes, in_specs=[SMEM] + [VMEM] *...  2.4 us
    pallas_call x1, Pallas kernels, load_inputs(): pl.pallas_call(functools.partial(load_kernel, tiles_count), out_shape=[pl...  1.61 us
    pallas_call x1, Pallas kernels, run_second(): pl.pallas_call(second_kernel, out_shape=[jax.ShapeDtypeStruct(array.shape...  1.16 us
    ppermute x1, waiting for transfers between devices, body(): packet = lax.ppermute(packet, 'sub', swap)  0.85 us
    ppermute x1, starting transfers between devices, body(): packet = lax.ppermute(packet, 'sub', swap)  0.52 us
  transfers between devices with their start and end apart: 3, of which 2 were waited for; matrix products, arithmetic and copies ran while one was open for 0% of the time, Pallas kernels for 42%

profile of v3, /device:TPU:0, one launch (start us, length us, event | category | flops | bytes accessed | tf_op | source)
XLA Modules:
  0.0 19.4 jit_solution(7832490284643153415)
XLA Ops:
  0.6 1.6 %load.1 = (s32[4]{0:T(128)S(4)}, f32[11,48,768]{2,1,0:T(8,128)S(1)}, s32[48,768]{1,0:T(8,128)S(1)}, f32[504,128]{1,0:T(8,128)S(1)}, f32[216,128]{1,0:T(8,128)S(1)}) custom-call(f32[48,768]{1,0:T(8,128)} %density.1, f32[3,48,768]{2,1,0:T(8,128)} %momentum.1, f32[6,48,768]{2,1,0:T(8,128)} %stress.1, f32[48,768]{1,0:T(8,128)} %red.1, s32[48,768]{1,0:T(8,128)} %solid.1, ...), custom_call_target="tpu_custom_call" | custom-call | tf_op jit(solution)/shard_map/load/pallas_call | solution.py:563
  2.3 0.5 %collective-permute-start = (f32[504,128]{1,0:T(8,128)S(1)}, f32[504,128]{1,0:T(8,128)S(1)}, u32[]{:S(2)}, u32[]{:S(2)}) collective-permute-start(f32[504,128]{1,0:T(8,128)S(1)} %get-tuple-element.27), channel_id=1, source_target_pairs={{0,1},{1,0},{2,3},{3,2},{4,5},{5,4},{6,7},{7,6},{8,9},{9,8},{10,11... | collective-permute-start | bytes 774152 | tf_op jit(solution)/shard_map/ppermute | solution.py:911
  2.8 0.3 %spread.1 = f32[48,104,128]{2,1,0:T(8,128)S(1)} custom-call(f32[11,48,768]{2,1,0:T(8,128)S(1)} %get-tuple-element.25.raw, s32[48,768]{1,0:T(8,128)S(1)} %get-tuple-element.26.raw_solid), custom_call_target="tpu_custom_call" | custom-call | flops 1000000 | bytes 4000000 | tf_op jit(solution)/shard_map/spread/pallas_call | solution.py:593
  3.1 0.9 %collective-permute-done.packet = f32[504,128]{1,0:T(8,128)S(1)} collective-permute-done((f32[504,128]{1,0:T(8,128)S(1)}, f32[504,128]{1,0:T(8,128)S(1)}, u32[]{:S(2)}, u32[]{:S(2)}) %collective-permute-start) | collective-permute-done | bytes 258080 | tf_op jit(solution)/shard_map/ppermute | solution.py:911
  3.9 4.8 %collective-permute-start.1 = (f32[432,128]{1,0:T(8,128)S(1)}, f32[432,128]{1,0:T(8,128)S(1)}, u32[]{:S(2)}, u32[]{:S(2)}) collective-permute-start(f32[432,128]{1,0:T(8,128)S(1)} %join.1), channel_id=1, source_target_pairs={{0,2},{2,4},{4,6},{6,8},{8,10},{10,12},{12,14},{3,1},{5,3},{7,5},{... | collective-permute-start | bytes 663560 | tf_op jit(solution)/shard_map/ppermute | solution.py:916
  8.8 0.1 beside.1.whole
  8.9 6.6 %first.1 = (f32[48,88,128]{2,1,0:T(8,128)S(1)}, f32[24,160,128]{2,1,0:T(8,128)S(1)}, f32[24,40,128]{2,1,0:T(8,128)S(1)}, f32[24,88,128]{2,1,0:T(8,128)S(1)}, f32...) custom-call(s32[4]{0:T(128)S(4)} %get-tuple-element.24.info, ...), custom_call_target="tpu_custom_call" | custom-call | flops 40000000 | bytes 8000000 | tf_op jit(solution)/shard_map/first/pallas_call | solution.py:766
  15.5 0.0 collective-permute-done.1.ends
  15.5 0.1 collective-permute-start.2
  15.6 1.2 %second.1 = (f32[48,768]{1,0:T(8,128)}, f32[3,48,768]{2,1,0:T(8,128)}, f32[6,48,768]{2,1,0:T(8,128)}, f32[48,768]{1,0:T(8,128)}) custom-call(s32[4]{0:T(128)S(4)} %get-tuple-element.24.info, f32[48,88,128]{2,1,0:T(8,128)S(1)} %get-tuple-element.35.final, f32[432,128]{1,0:T(8,128)S(1)} %follow.1.arrived), custom_call_target="tpu_custom_call" | custom-call | flops 20000000 | bytes 8000000 | tf_op jit(solution)/shard_map/second/pallas_call | solution.py:781
  16.8 0.3 %collective-permute-done.2.passed = f32[432,128]{1,0:T(8,128)S(1)} collective-permute-done((f32[432,128]{1,0:T(8,128)S(1)}, f32[432,128]{1,0:T(8,128)S(1)}, u32[]{:S(2)}, u32[]{:S(2)}) %collective-permute-start.2) | collective-permute-done | bytes 221216 | tf_op jit(solution)/shard_map/ppermute | solution.py:920
  17.0 2.4 %outer.1 = (f32[48,768]{1,0:T(8,128)}, f32[3,48,768]{2,1,0:T(8,128)}, f32[6,48,768]{2,1,0:T(8,128)}, f32[48,768]{1,0:T(8,128)}, f32[24,160,128]{2,1,0:T(8,128)S(...) custom-call(s32[4]{0:T(128)S(4)} %get-tuple-element.24.info, ...), custom_call_target="tpu_custom_call", output_to_operand_aliasing={{4}: (4, {}), {5}: (5, {}), {6}: (6, {}), {7}: (7, {}), {8}... | custom-call | tf_op jit(solution)/shard_map/outer/pallas_call | solution.py:887
  (2 shorter events, 0.0 us)
Async XLA Ops:
  2.3 1.7 %collective-permute-start = (f32[504,128]{1,0:T(8,128)S(1)}, f32[504,128]{1,0:T(8,128)S(1)}, u32[]{:S(2)}, u32[]{:S(2)}) collective-permute-start(f32[504,128]{1,0:T(8,128)S(1)} %get-tuple-element.27), channel_id=1, source_target_pairs={{0,1},{1,0},{2,3},{3,2},{4,5},{5,4},{6,7},{7,6},{8,9},{9,8},{10,11... | collective-permute-start | bytes 774152 | tf_op jit(solution)/shard_map/ppermute | solution.py:911
  3.9 11.5 %collective-permute-start.1 = (f32[432,128]{1,0:T(8,128)S(1)}, f32[432,128]{1,0:T(8,128)S(1)}, u32[]{:S(2)}, u32[]{:S(2)}) collective-permute-start(f32[432,128]{1,0:T(8,128)S(1)} %join.1), channel_id=1, source_target_pairs={{0,2},{2,4},{4,6},{6,8},{8,10},{10,12},{12,14},{3,1},{5,3},{7,5},{... | collective-permute-start | bytes 663560 | tf_op jit(solution)/shard_map/ppermute | solution.py:916
  15.5 1.5 %collective-permute-start.2 = (f32[432,128]{1,0:T(8,128)S(1)}, f32[432,128]{1,0:T(8,128)S(1)}, u32[]{:S(2)}, u32[]{:S(2)}) collective-permute-start(f32[432,128]{1,0:T(8,128)S(1)} %follow.1.arrived), channel_id=1, source_target_pairs={{0,1},{1,0},{2,3},{3,2},{4,5},{5,4},{6,7},{7,6},{8,9},{9,8},{10,11... | collective-permute-start | bytes 663560 | tf_op jit(solution)/shard_map/ppermute | solution.py:920

commit v4 on v3

--- a/solution.py
+++ b/solution.py
@@ -693,8 +693,8 @@
 
 def first_kernel(
     info, whole, final,
-    moved_slab, reds_slab, fields_slab, moved_later_slab, reds_later_slab, final_slab,
-    colours, walls, moved, reds, fields, moved_later, reds_later,
+    moved_slab, reds_slab, fields_slab, moved_later_slab, reds_later_slab, start_slab, walls, final_slab,
+    colours, moved, reds, fields, moved_later, reds_later,
 ):
     state, later = (ByRow(moved), ByRow(reds)), (ByRow(moved_later), ByRow(reds_later))
     geometry = Geometry(info, OWN_TILES)
@@ -703,6 +703,7 @@
     collide_rows(geometry, ByRow(whole), ByRow(whole), 1, ByRow(colours), walls, state)
     over_rows(geometry, 2, *ARRIVE_BLOCK, lambda block: arrive_stage(
         block, geometry, walls, state, ByRow(fields)))
+    keep_rows(start_slab, whole, HALO, FULL, live)
     keep_rows(moved_slab, moved, HALO + 1, KEPT, live)
     keep_rows(reds_slab, reds, HALO + 1, KEPT, live)
     keep_rows(fields_slab, fields, HALO + 2, KEPT, live)
@@ -760,14 +761,15 @@
 
 def run_first(info, whole):
     rows = whole.shape[0]
-    slabs = [by_row(2 * SLAB, count) for count in (HELD, REDS, FIELDS, HELD, REDS, FIELDS)]
-    scratch = [by_row(rows, 4), by_row(4, 3)]
+    slabs = [by_row(2 * SLAB, count) for count in (HELD, REDS, FIELDS, HELD, REDS, PLACES)]
+    slabs = slabs + [by_row(4, 3), by_row(2 * SLAB, FIELDS)]
+    scratch = [by_row(rows, 4)]
     scratch = scratch + [by_row(rows, count) for count in (HELD, REDS, FIELDS, HELD, REDS)]
     return pl.pallas_call(
         first_kernel,
         out_shape=[by_row(rows, FIELDS)] + slabs,
         in_specs=[SMEM, VMEM],
-        out_specs=[VMEM] * 7,
+        out_specs=[VMEM] * 9,
         scratch_shapes=[scratch_of(shape) for shape in scratch],
         compiler_params=pltpu.CompilerParams(vmem_limit_bytes=32 * 1024 * 1024),
         cost_estimate=pl.CostEstimate(flops=40_000_000, bytes_accessed=8_000_000, transcendentals=0),
@@ -809,15 +811,14 @@
     )(pltpu.with_memory_space_constraint(ends, pltpu.VMEM), kept)
 
 
-def outer_kernel(info, whole, arrived, passed, *refs):
-    outs = refs[10:14]
-    moved, reds, fields, moved_later, reds_later, final = refs[14:20]
-    start_fields, colours, walls, pieces, sems = refs[20:]
+def outer_kernel(info, arrived, passed, *refs):
+    outs = refs[12:16]
+    moved, reds, fields, moved_later, reds_later, start_fields, walls, final = refs[16:24]
+    colours, pieces, sems = refs[24:]
     state, later = (ByRow(moved), ByRow(reds)), (ByRow(moved_later), ByRow(reds_later))
     geometry = Geometry(info, OWN_TILES)
     live = geometry.live
     low_part = info[3] == 0
-    fill_wall_table(walls, geometry)
 
     def ends_of(ref, half):
         blocks = []
@@ -850,10 +851,6 @@
         write_row(ByRow(start_fields), SPARE, next_row, jnp.zeros((SUBLANES, LANES), jnp.float32))
         write_row(ByRow(start_fields), 0, row, jnp.zeros((SUBLANES, LANES), jnp.float32))
         write_row(ByRow(start_fields), 10, row, 0.5 * colour)
-    for slab_row, row in slab_rows(live, HALO, FULL):
-        for extra in range(FULL):
-            start_fields[slab_row + extra] = whole[row + extra]
-
     def block(first, count):
         return Block(geometry, [(row, at, count) for at, row in slab_rows(live, first, count)])
 
@@ -869,37 +866,34 @@
     for side, row, out_row in ((0, HALO, 0), (1, SLAB, live - SUBLANES)):
         gather_tiles(final, row, pieces, side * SUBLANES)
         out_row = pl.multiple_of(out_row, SUBLANES)
-        copies = copies + row_copies(
-            pieces, outs, side * SUBLANES, out_row, SUBLANES, sems.at[side]
-        )
-    for copy in copies:
-        copy.start()
+        started = row_copies(pieces, outs, side * SUBLANES, out_row, SUBLANES, sems.at[side])
+        for copy in started:
+            copy.start()
+        copies = copies + started
     for copy in copies:
         copy.wait()
 
 
-def run_outer(info, whole, arrived, passed, slabs, outs):
+def run_outer(info, arrived, passed, slabs, outs):
     flat_count = outs[0].shape[1]
     shapes = [jax.ShapeDtypeStruct(array.shape, jnp.float32) for array in (*outs, *slabs)]
     slabs = [pltpu.with_memory_space_constraint(slab, pltpu.VMEM) for slab in slabs]
-    aliases = {4 + number: 4 + number for number in range(6)}
-    aliases.update({10 + number: number for number in range(4)})
+    aliases = {3 + number: 4 + number for number in range(8)}
+    aliases.update({11 + number: number for number in range(4)})
     return pl.pallas_call(
         outer_kernel,
         out_shape=shapes,
-        in_specs=[SMEM] + [VMEM] * 9 + [ANY] * 4,
-        out_specs=[ANY] * 4 + [VMEM] * 6,
+        in_specs=[SMEM] + [VMEM] * 10 + [ANY] * 4,
+        out_specs=[ANY] * 4 + [VMEM] * 8,
         scratch_shapes=[
-            scratch_of(by_row(2 * SLAB, PLACES)),
             scratch_of(by_row(2 * SLAB, 4)),
-            scratch_of(by_row(4, 3)),
             pieces_of(2 * SUBLANES, flat_count),
             pltpu.SemaphoreType.DMA((2, OUT_COPIES)),
         ],
         input_output_aliases=aliases,
         compiler_params=pltpu.CompilerParams(vmem_limit_bytes=24 * 1024 * 1024),
         name="outer",
-    )(info, whole, arrived, passed, *slabs, *outs)
+    )(info, arrived, passed, *slabs, *outs)
 
 
 def body(density, momentum, stress, red_density, solid, widths):
@@ -919,7 +913,7 @@
     arrived = follow(arrived, slabs[-1])
     passed = lax.ppermute(arrived, "sub", swap)
     outs = run_second(info, final, arrived, arrays)
-    return tuple(run_outer(info, whole, arrived, passed, slabs, outs)[:4])
+    return tuple(run_outer(info, arrived, passed, slabs, outs)[:4])
 
 
 def solution(mesh):

time: 19.6 us -> 18.5 us (0.944)
  Pallas kernels: 12.2 us -> 9.81 us
  waiting for transfers between devices: 1.15 us -> 2.53 us
    pallas_call x1, Pallas kernels: 6.6 us -> 4.29 us  [run_first(): pl.pallas_call(first_kernel, out_shape=[by_row(rows, FIELDS)] + slabs, in...]
    ppermute x1, waiting for transfers between devices: 0.01 us -> 1.37 us  [body(): arrived = lax.ppermute(ends, ('tiles', 'sub'), route)]
  transfers between devices with their start and end apart: 3 -> 3, of which waited for: 2 -> 3; matrix products, arithmetic and copies ran while one was open for 0% -> 0% of each run, Pallas kernels for 42% -> 32%
where the time goes in v4:
time: 18.5 us; the launch traced here: 18.3 us
  Pallas kernels  9.81 us (53%)
  starting transfers between devices  5.33 us (29%)
  waiting for transfers between devices  2.53 us (14%)
  between operations  0.68 us (4%)
    ppermute x1, starting transfers between devices, body(): arrived = lax.ppermute(ends, ('tiles', 'sub'), route)  4.81 us
    pallas_call x1, Pallas kernels, run_first(): pl.pallas_call(first_kernel, out_shape=[by_row(rows, FIELDS)] + slabs, in...  4.29 us
    pallas_call x1, Pallas kernels, run_outer(): pl.pallas_call(outer_kernel, out_shape=shapes, in_specs=[SMEM] + [VMEM] *...  2.32 us
    pallas_call x1, Pallas kernels, load_inputs(): pl.pallas_call(functools.partial(load_kernel, tiles_count), out_shape=[pl...  1.61 us
    ppermute x1, waiting for transfers between devices, body(): arrived = lax.ppermute(ends, ('tiles', 'sub'), route)  1.37 us
    pallas_call x1, Pallas kernels, run_second(): pl.pallas_call(second_kernel, out_shape=[jax.ShapeDtypeStruct(array.shape...  1.15 us
    ppermute x1, waiting for transfers between devices, body(): packet = lax.ppermute(packet, 'sub', swap)  0.85 us
    ppermute x1, starting transfers between devices, body(): packet = lax.ppermute(packet, 'sub', swap)  0.52 us
  transfers between devices with their start and end apart: 3, of which 3 were waited for; matrix products, arithmetic and copies ran while one was open for 0% of the time, Pallas kernels for 32%

profile of v4, /device:TPU:0, one launch (start us, length us, event | category | flops | bytes accessed | tf_op | source)
XLA Modules:
  0.0 18.3 jit_solution(12916243960309483524)
XLA Ops:
  0.6 1.6 %load.1 = (s32[4]{0:T(128)S(4)}, f32[11,48,768]{2,1,0:T(8,128)S(1)}, s32[48,768]{1,0:T(8,128)S(1)}, f32[504,128]{1,0:T(8,128)S(1)}, f32[216,128]{1,0:T(8,128)S(1)}) custom-call(f32[48,768]{1,0:T(8,128)} %density.1, f32[3,48,768]{2,1,0:T(8,128)} %momentum.1, f32[6,48,768]{2,1,0:T(8,128)} %stress.1, f32[48,768]{1,0:T(8,128)} %red.1, s32[48,768]{1,0:T(8,128)} %solid.1, ...), custom_call_target="tpu_custom_call" | custom-call | tf_op jit(solution)/shard_map/load/pallas_call | solution.py:563
  2.3 0.5 %collective-permute-start = (f32[504,128]{1,0:T(8,128)S(1)}, f32[504,128]{1,0:T(8,128)S(1)}, u32[]{:S(2)}, u32[]{:S(2)}) collective-permute-start(f32[504,128]{1,0:T(8,128)S(1)} %get-tuple-element.28), channel_id=1, source_target_pairs={{0,1},{1,0},{2,3},{3,2},{4,5},{5,4},{6,7},{7,6},{8,9},{9,8},{10,11... | collective-permute-start | bytes 774152 | tf_op jit(solution)/shard_map/ppermute | solution.py:905
  2.8 0.3 %spread.1 = f32[48,104,128]{2,1,0:T(8,128)S(1)} custom-call(f32[11,48,768]{2,1,0:T(8,128)S(1)} %get-tuple-element.29.raw, s32[48,768]{1,0:T(8,128)S(1)} %get-tuple-element.30.raw_solid), custom_call_target="tpu_custom_call" | custom-call | flops 1000000 | bytes 4000000 | tf_op jit(solution)/shard_map/spread/pallas_call | solution.py:593
  3.1 0.9 %collective-permute-done.packet = f32[504,128]{1,0:T(8,128)S(1)} collective-permute-done((f32[504,128]{1,0:T(8,128)S(1)}, f32[504,128]{1,0:T(8,128)S(1)}, u32[]{:S(2)}, u32[]{:S(2)}) %collective-permute-start) | collective-permute-done | bytes 258080 | tf_op jit(solution)/shard_map/ppermute | solution.py:905
  3.9 4.8 %collective-permute-start.1 = (f32[432,128]{1,0:T(8,128)S(1)}, f32[432,128]{1,0:T(8,128)S(1)}, u32[]{:S(2)}, u32[]{:S(2)}) collective-permute-start(f32[432,128]{1,0:T(8,128)S(1)} %join.1), channel_id=1, source_target_pairs={{0,2},{2,4},{4,6},{6,8},{8,10},{10,12},{12,14},{3,1},{5,3},{7,5},{... | collective-permute-start | bytes 663560 | tf_op jit(solution)/shard_map/ppermute | solution.py:910
  8.8 0.1 beside.1.whole
  8.9 4.3 %first.1 = (f32[48,88,128]{2,1,0:T(8,128)S(1)}, f32[24,160,128]{2,1,0:T(8,128)S(1)}, f32[24,40,128]{2,1,0:T(8,128)S(1)}, f32[24,88,128]{2,1,0:T(8,128)S(1)}, f32...) custom-call(s32[4]{0:T(128)S(4)} %get-tuple-element.26.info, ...), custom_call_target="tpu_custom_call" | custom-call | flops 40000000 | bytes 8000000 | tf_op jit(solution)/shard_map/first/pallas_call | solution.py:768
  13.2 1.4 %collective-permute-done.1.ends = f32[432,128]{1,0:T(8,128)S(1)} collective-permute-done((f32[432,128]{1,0:T(8,128)S(1)}, f32[432,128]{1,0:T(8,128)S(1)}, u32[]{:S(2)}, u32[]{:S(2)}) %collective-permute-start.1) | collective-permute-done | bytes 221216 | tf_op jit(solution)/shard_map/ppermute | solution.py:910
  14.6 0.0 collective-permute-start.2
  14.6 1.2 %second.1 = (f32[48,768]{1,0:T(8,128)}, f32[3,48,768]{2,1,0:T(8,128)}, f32[6,48,768]{2,1,0:T(8,128)}, f32[48,768]{1,0:T(8,128)}) custom-call(s32[4]{0:T(128)S(4)} %get-tuple-element.26.info, f32[48,88,128]{2,1,0:T(8,128)S(1)} %get-tuple-element.39.final, f32[432,128]{1,0:T(8,128)S(1)} %follow.1.arrived), custom_call_target="tpu_custom_call" | custom-call | flops 20000000 | bytes 8000000 | tf_op jit(solution)/shard_map/second/pallas_call | solution.py:783
  15.7 0.3 %collective-permute-done.2.passed = f32[432,128]{1,0:T(8,128)S(1)} collective-permute-done((f32[432,128]{1,0:T(8,128)S(1)}, f32[432,128]{1,0:T(8,128)S(1)}, u32[]{:S(2)}, u32[]{:S(2)}) %collective-permute-start.2) | collective-permute-done | bytes 221216 | tf_op jit(solution)/shard_map/ppermute | solution.py:914
  16.0 2.3 %outer.1 = (f32[48,768]{1,0:T(8,128)}, f32[3,48,768]{2,1,0:T(8,128)}, f32[6,48,768]{2,1,0:T(8,128)}, f32[48,768]{1,0:T(8,128)}, f32[24,160,128]{2,1,0:T(8,128)S(...) custom-call(s32[4]{0:T(128)S(4)} %get-tuple-element.26.info, ...), custom_call_target="tpu_custom_call", output_to_operand_aliasing={{4}: (3, {}), {5}: (4, {}), {6}: (5, {}), {7}: (6, {}), {8}... | custom-call | tf_op jit(solution)/shard_map/outer/pallas_call | solution.py:883
  (2 shorter events, 0.0 us)
Async XLA Ops:
  2.3 1.7 %collective-permute-start = (f32[504,128]{1,0:T(8,128)S(1)}, f32[504,128]{1,0:T(8,128)S(1)}, u32[]{:S(2)}, u32[]{:S(2)}) collective-permute-start(f32[504,128]{1,0:T(8,128)S(1)} %get-tuple-element.28), channel_id=1, source_target_pairs={{0,1},{1,0},{2,3},{3,2},{4,5},{5,4},{6,7},{7,6},{8,9},{9,8},{10,11... | collective-permute-start | bytes 774152 | tf_op jit(solution)/shard_map/ppermute | solution.py:905
  3.9 10.6 %collective-permute-start.1 = (f32[432,128]{1,0:T(8,128)S(1)}, f32[432,128]{1,0:T(8,128)S(1)}, u32[]{:S(2)}, u32[]{:S(2)}) collective-permute-start(f32[432,128]{1,0:T(8,128)S(1)} %join.1), channel_id=1, source_target_pairs={{0,2},{2,4},{4,6},{6,8},{8,10},{10,12},{12,14},{3,1},{5,3},{7,5},{... | collective-permute-start | bytes 663560 | tf_op jit(solution)/shard_map/ppermute | solution.py:910
  14.6 1.5 %collective-permute-start.2 = (f32[432,128]{1,0:T(8,128)S(1)}, f32[432,128]{1,0:T(8,128)S(1)}, u32[]{:S(2)}, u32[]{:S(2)}) collective-permute-start(f32[432,128]{1,0:T(8,128)S(1)} %follow.1.arrived), channel_id=1, source_target_pairs={{0,1},{1,0},{2,3},{3,2},{4,5},{5,4},{6,7},{7,6},{8,9},{9,8},{10,11... | collective-permute-start | bytes 663560 | tf_op jit(solution)/shard_map/ppermute | solution.py:914
